TPU v7x, 512 devices: a whole 4x8x8 slice. The times are simulated.
512 devices in a mesh: task: 128 (over z, y, core), aux: 4 (over x).
Axes of the slice: x: 4, y: 8, z: 8, core: 2. Of those that a mesh axis runs over, the one named last changes fastest.
Arguments:
- factors: bfloat16 [128, 2048, 1024], P('task', 'aux'), may hold values from -0.125 to 0.125
- amplitudes: bfloat16 [128, 256, 1024], P('task'), may hold values from -6 to 6
- task_counts: int32 [128], P('task'), may hold values from 1 to 4, 256 in all
- task_tiles: int32 [128, 4, 3], P('task'), may hold values from 0 to 4
Outputs:
- residual: float32 [128, 256, 1024], P('task', None, 'aux')
Inputs may be any that keep to these rules, and one draw needn't show every extreme that they name: `task_counts`: every tile has 1 to 4 tasks, exactly 256 in all; some tile has exactly 4.
All inputs are finite; a program needn't handle non-finite values. No bound on the sum of `task_counts` on one device may be relied on, other than what follows from the above.
Results may differ from a plain program's by a relative error of at most 0.0026.
Values may be sent and summed in bfloat16 or wider, within the bound.
No kernel may reach another device: no remote copies, remote signals or barrier semaphores. Data moves between devices by JAX's collectives and lax.ppermute only.
A program may use at most 64 MiB of HBM per device.

v0:
```python
import jax
import jax.numpy as jnp
from jax import lax
from jax.sharding import PartitionSpec as P

VB = 32
RADIUS = 2


def shifted(block, axis, distance):
    devices = range(lax.axis_size(axis))
    route = [((i - distance) % len(devices), i) for i in devices]
    return lax.ppermute(block, axis, route)


def split_up(shard, dim, peers):
    before, after = (shard.shape[:dim], shard.shape[dim + 1 :])
    return jnp.moveaxis(shard.reshape(*before, peers, -1, *after), dim, 0)


def summed_on_arrival(shard, axis, dim):
    peers = lax.axis_size(axis)
    parts = lax.all_to_all(split_up(shard, dim, peers), axis, 0, 0, tiled=True)
    return jnp.sum(parts, axis=0)


def task_term(first, second, amp, width):
    tile = lax.dot_general(
        first, second, (((0,), (0,)), ((), ())), preferred_element_type=jnp.float32
    )
    tile = (
        tile.reshape(width, width, width, width)
        .transpose(1, 3, 0, 2)
        .reshape(width * width, width * width)
    )
    tile = tile.astype(jnp.bfloat16)
    return jnp.dot(amp, tile, preferred_element_type=jnp.float32)


def run_tasks(window_fac, window_amp, plan, first, last, centre, lowest, width):

    def one_task(slot, total):
        offs = lax.dynamic_index_in_dim(plan, slot, 0, False) - RADIUS + centre - lowest
        left = lax.dynamic_index_in_dim(window_fac, offs[0], 0, False)
        right = lax.dynamic_index_in_dim(window_fac, offs[1], 0, False)
        amp = lax.dynamic_index_in_dim(window_amp, offs[2], 0, False)
        return total + task_term(left, right, amp, width)

    start = jnp.zeros((window_amp.shape[1], window_amp.shape[2]), jnp.float32)
    return lax.fori_loop(first, last, one_task, start)


def shards(factors, amplitudes, task_counts, task_tiles):
    width = VB
    own_fac = factors[0]
    own_amp = amplitudes[0]
    fac_list = []
    amp_list = []
    for offset in range(-RADIUS, RADIUS + 1):
        if offset == 0:
            fac_list.append(own_fac)
            amp_list.append(own_amp)
        else:
            moved = shifted((own_fac, own_amp), "task", -offset)
            fac_list.append(moved[0])
            amp_list.append(moved[1])
    window_fac = jnp.stack(fac_list)
    window_amp = jnp.stack(amp_list)
    partial_sum = run_tasks(
        window_fac, window_amp, task_tiles[0], 0, task_counts[0], 0, -RADIUS, width
    )
    summed = summed_on_arrival(partial_sum, "aux", 1)
    return summed[None]


def solution(mesh):
    return jax.shard_map(
        shards,
        mesh=mesh,
        in_specs=(P("task", "aux", None), P("task", None, None), P("task"), P("task", None, None)),
        out_specs=P("task", None, "aux"),
        check_vma=False,
    )
```

profile of v0, /device:TPU:448, one launch (start us, length us, event | category | flops | bytes accessed | tf_op | source)
XLA Modules:
  0.0 196.3 jit_solution(6366474945505609941)
XLA Ops:
  0.0 3.6 %collective-permute-start = (bf16[256,1024]{1,0:T(8,128)(2,1)}, bf16[256,1024]{1,0:T(8,128)(2,1)}, u32[]{:S(2)}, u32[]{:S(2)}) collective-permute-start(bf16[256,1024]{1,0:T(8,128)(2,1)} %bitcast.82), channel_id=1, source_target_pairs={{504,0},{508,4},{0,8},{4,12},{8,16},{12,20},{16,24},{20,28},{24,32... | collective-permute-start | bytes 1572872 | tf_op jit(solution)/shard_map/ppermute | solution.py:13
  3.6 1.9 collective-permute-start.1
  5.5 4.5 %collective-permute-start.3 = (bf16[256,1024]{1,0:T(8,128)(2,1)}, bf16[256,1024]{1,0:T(8,128)(2,1)S(1)}, u32[]{:S(2)}, u32[]{:S(2)}) collective-permute-start(bf16[256,1024]{1,0:T(8,128)(2,1)} %bitcast.84), channel_id=1, source_target_pairs={{8,0},{12,4},{16,8},{20,12},{24,16},{28,20},{32,24},{36,28},{40,32... | collective-permute-start | bytes 1572872 | tf_op jit(solution)/shard_map/ppermute | solution.py:13
  10.0 3.4 %collective-permute-start.2 = (bf16[256,1024]{1,0:T(8,128)(2,1)}, bf16[256,1024]{1,0:T(8,128)(2,1)}, u32[]{:S(2)}, u32[]{:S(2)}) collective-permute-start(bf16[256,1024]{1,0:T(8,128)(2,1)} %bitcast.85), channel_id=1, source_target_pairs={{4,0},{8,4},{12,8},{16,12},{20,16},{24,20},{28,24},{32,28},{36,32}... | collective-permute-start | bytes 1572872 | tf_op jit(solution)/shard_map/ppermute | solution.py:13
  13.4 1.5 copy.12
  14.9 3.3 %collective-permute-start.7 = (bf16[512,1024]{0,1:T(8,128)(2,1)S(1)}, bf16[512,1024]{0,1:T(8,128)(2,1)S(1)}, u32[]{:S(2)}, u32[]{:S(2)}) collective-permute-start(bf16[512,1024]{0,1:T(8,128)(2,1)S(1)} %bitcast.77), channel_id=1, source_target_pairs={{8,0},{12,4},{16,8},{20,12},{24,16},{28,20},{32,24},{36,28},{40,32... | collective-permute-start | bytes 3145736 | tf_op jit(solution)/shard_map/ppermute | solution.py:13
  19.3 2.3 %collective-permute-start.4 = (bf16[512,1024]{0,1:T(8,128)(2,1)S(1)}, bf16[512,1024]{0,1:T(8,128)(2,1)S(1)}, u32[]{:S(2)}, u32[]{:S(2)}) collective-permute-start(bf16[512,1024]{0,1:T(8,128)(2,1)S(1)} %bitcast.78), channel_id=1, source_target_pairs={{504,0},{508,4},{0,8},{4,12},{8,16},{12,20},{16,24},{20,28},{24,32... | collective-permute-start | bytes 3145736 | tf_op jit(solution)/shard_map/ppermute | solution.py:13
  23.7 1.9 collective-permute-start.5
  26.8 6.4 %collective-permute-done.2 = bf16[256,1024]{1,0:T(8,128)(2,1)} collective-permute-done((bf16[256,1024]{1,0:T(8,128)(2,1)}, bf16[256,1024]{1,0:T(8,128)(2,1)}, u32[]{:S(2)}, u32[]{:S(2)}) %collective-permute-start.2) | collective-permute-done | bytes 524320 | tf_op jit(solution)/shard_map/ppermute | solution.py:13
  33.2 5.9 %collective-permute-start.6 = (bf16[512,1024]{0,1:T(8,128)(2,1)S(1)}, bf16[512,1024]{0,1:T(8,128)(2,1)S(1)}, u32[]{:S(2)}, u32[]{:S(2)}) collective-permute-start(bf16[512,1024]{0,1:T(8,128)(2,1)S(1)} %bitcast.80), channel_id=1, source_target_pairs={{4,0},{8,4},{12,8},{16,12},{20,16},{24,20},{28,24},{32,28},{36,32}... | collective-permute-start | bytes 3145736 | tf_op jit(solution)/shard_map/ppermute | solution.py:13
  41.7 7.6 %collective-permute-done.4 = bf16[512,1024]{0,1:T(8,128)(2,1)S(1)} collective-permute-done((bf16[512,1024]{0,1:T(8,128)(2,1)S(1)}, bf16[512,1024]{0,1:T(8,128)(2,1)S(1)}, u32[]{:S(2)}, u32[]{:S(2)}) %collective-permute-start.4) | collective-permute-done | bytes 1048608 | tf_op jit(solution)/shard_map/ppermute | solution.py:13
  49.4 8.6 %collective-permute-done.5 = bf16[512,1024]{0,1:T(8,128)(2,1)S(1)} collective-permute-done((bf16[512,1024]{0,1:T(8,128)(2,1)S(1)}, bf16[512,1024]{0,1:T(8,128)(2,1)S(1)}, u32[]{:S(2)}, u32[]{:S(2)}) %collective-permute-start.5) | collective-permute-done | bytes 1048608 | tf_op jit(solution)/shard_map/ppermute | solution.py:13
  58.2 3.7 %collective-permute-done.6 = bf16[512,1024]{0,1:T(8,128)(2,1)S(1)} collective-permute-done((bf16[512,1024]{0,1:T(8,128)(2,1)S(1)}, bf16[512,1024]{0,1:T(8,128)(2,1)S(1)}, u32[]{:S(2)}, u32[]{:S(2)}) %collective-permute-start.6) | collective-permute-done | bytes 1048608 | tf_op jit(solution)/shard_map/ppermute | solution.py:13
  62.1 2.3 %copy-done = bf16[5,512,1024]{1,2,0:T(8,128)(2,1)} copy-done((bf16[5,512,1024]{1,2,0:T(8,128)(2,1)}, bf16[5,512,1024]{1,2,0:T(8,128)(2,1)S(1)}, u32[]{:S(2)}) %copy-start) | copy-done | bytes 5242904
  64.4 115.5 %while.14 = (s32[]{:T(128)}, f32[256,1024]{1,0:T(8,128)S(1)}, s32[]{:T(128)}, s32[4,3]{1,0:T(4,128)S(1)}, bf16[5,256,1024]{2,1,0:T(8,128)(2,1)}, /*index=5*/bf16...) while((s32[]{:T(128)}, f32[256,1024]{1,0:T(8,128)S(1)}, s32[]{:T(128)}, ...), condition=%wide.region_1.2_spmd, body=%wide.region_0.1_spmd.sunk | while | flops 1611923456 | bytes 17301812 | solution.py:50
  71.2 1.7 constant_dynamic-slice_fusion.6
  72.9 7.0 %convert_bitcast_fusion.2 = bf16[32,32,32,32]{1,0,3,2:T(8,128)(2,1)} fusion(bf16[32,32,512,1]{2,1,3,0:T(8,128)(2,1)S(1)} %bitcast.76, bf16[32,32,512,1]{2,1,0,3:T(8,128)(2,1)S(1)} %bitcast.75), kind=kOutput, calls=%fused_computation.clone.1 | convolution fusion | flops 1074790400 | bytes 4194304 | tf_op jit(solution)/shard_map/while/body/dot_general | solution.py:28
  79.9 11.3 %convert_element_type.19 = bf16[1024,1024]{0,1:T(8,128)(2,1)S(1)} reshape(bf16[32,32,32,32]{1,0,3,2:T(8,128)(2,1)} %convert_bitcast_fusion.2) | data formatting | bytes 4194304 | tf_op jit(solution)/shard_map/while/body/convert_element_type | solution.py:36
  91.2 1.9 convolution_add_fusion.2
  99.9 1.7 constant_dynamic-slice_fusion.6
  101.6 7.0 %convert_bitcast_fusion.2 = bf16[32,32,32,32]{1,0,3,2:T(8,128)(2,1)} fusion(bf16[32,32,512,1]{2,1,3,0:T(8,128)(2,1)S(1)} %bitcast.76, bf16[32,32,512,1]{2,1,0,3:T(8,128)(2,1)S(1)} %bitcast.75), kind=kOutput, calls=%fused_computation.clone.1 | convolution fusion | flops 1074790400 | bytes 4194304 | tf_op jit(solution)/shard_map/while/body/dot_general | solution.py:28
  108.6 11.3 %convert_element_type.19 = bf16[1024,1024]{0,1:T(8,128)(2,1)S(1)} reshape(bf16[32,32,32,32]{1,0,3,2:T(8,128)(2,1)} %convert_bitcast_fusion.2) | data formatting | bytes 4194304 | tf_op jit(solution)/shard_map/while/body/convert_element_type | solution.py:36
  119.9 1.9 convolution_add_fusion.2
  128.6 1.7 constant_dynamic-slice_fusion.6
  130.3 7.0 %convert_bitcast_fusion.2 = bf16[32,32,32,32]{1,0,3,2:T(8,128)(2,1)} fusion(bf16[32,32,512,1]{2,1,3,0:T(8,128)(2,1)S(1)} %bitcast.76, bf16[32,32,512,1]{2,1,0,3:T(8,128)(2,1)S(1)} %bitcast.75), kind=kOutput, calls=%fused_computation.clone.1 | convolution fusion | flops 1074790400 | bytes 4194304 | tf_op jit(solution)/shard_map/while/body/dot_general | solution.py:28
  137.3 11.3 %convert_element_type.19 = bf16[1024,1024]{0,1:T(8,128)(2,1)S(1)} reshape(bf16[32,32,32,32]{1,0,3,2:T(8,128)(2,1)} %convert_bitcast_fusion.2) | data formatting | bytes 4194304 | tf_op jit(solution)/shard_map/while/body/convert_element_type | solution.py:36
  148.6 1.9 convolution_add_fusion.2
  157.3 1.7 constant_dynamic-slice_fusion.6
  159.0 7.0 %convert_bitcast_fusion.2 = bf16[32,32,32,32]{1,0,3,2:T(8,128)(2,1)} fusion(bf16[32,32,512,1]{2,1,3,0:T(8,128)(2,1)S(1)} %bitcast.76, bf16[32,32,512,1]{2,1,0,3:T(8,128)(2,1)S(1)} %bitcast.75), kind=kOutput, calls=%fused_computation.clone.1 | convolution fusion | flops 1074790400 | bytes 4194304 | tf_op jit(solution)/shard_map/while/body/dot_general | solution.py:28
  166.0 11.3 %convert_element_type.19 = bf16[1024,1024]{0,1:T(8,128)(2,1)S(1)} reshape(bf16[32,32,32,32]{1,0,3,2:T(8,128)(2,1)} %convert_bitcast_fusion.2) | data formatting | bytes 4194304 | tf_op jit(solution)/shard_map/while/body/convert_element_type | solution.py:36
  177.3 1.9 convolution_add_fusion.2
  180.6 15.0 %all_to_all.5 = f32[4,256,256]{2,1,0:T(8,128)S(1)} all-to-all(f32[4,256,256]{2,1,0:T(8,128)S(1)} %copy.15), channel_id=1, replica_groups=mesh['task'=128,'aux'=4] {'aux'}, dimensions={0} | all-to-all | bytes 2097152 | tf_op jit(solution)/shard_map/all_to_all | solution.py:23
  (32 shorter events, 11.6 us)
Async XLA Ops:
  0.0 26.7 %copy-start.2 = (bf16[1,256,1024]{2,1,0:T(8,128)(2,1)S(1)}, bf16[1,256,1024]{2,1,0:T(8,128)(2,1)}, u32[]{:S(2)}) copy-start(bf16[1,256,1024]{2,1,0:T(8,128)(2,1)} %param.7) | copy-start | bytes 1572868
  0.0 19.2 %collective-permute-start = (bf16[256,1024]{1,0:T(8,128)(2,1)}, bf16[256,1024]{1,0:T(8,128)(2,1)}, u32[]{:S(2)}, u32[]{:S(2)}) collective-permute-start(bf16[256,1024]{1,0:T(8,128)(2,1)} %bitcast.82), channel_id=1, source_target_pairs={{504,0},{508,4},{0,8},{4,12},{8,16},{12,20},{16,24},{20,28},{24,32... | collective-permute-start | bytes 1572872 | tf_op jit(solution)/shard_map/ppermute | solution.py:13
  3.6 20.1 %collective-permute-start.1 = (bf16[256,1024]{1,0:T(8,128)(2,1)}, bf16[256,1024]{1,0:T(8,128)(2,1)}, u32[]{:S(2)}, u32[]{:S(2)}) collective-permute-start(bf16[256,1024]{1,0:T(8,128)(2,1)} %bitcast.83), channel_id=1, source_target_pairs={{508,0},{0,4},{4,8},{8,12},{12,16},{16,20},{20,24},{24,28},{28,32}... | collective-permute-start | bytes 1572872 | tf_op jit(solution)/shard_map/ppermute | solution.py:13
  5.5 34.7 %collective-permute-start.3 = (bf16[256,1024]{1,0:T(8,128)(2,1)}, bf16[256,1024]{1,0:T(8,128)(2,1)S(1)}, u32[]{:S(2)}, u32[]{:S(2)}) collective-permute-start(bf16[256,1024]{1,0:T(8,128)(2,1)} %bitcast.84), channel_id=1, source_target_pairs={{8,0},{12,4},{16,8},{20,12},{24,16},{28,20},{32,24},{36,28},{40,32... | collective-permute-start | bytes 1572872 | tf_op jit(solution)/shard_map/ppermute | solution.py:13
  10.0 23.2 %collective-permute-start.2 = (bf16[256,1024]{1,0:T(8,128)(2,1)}, bf16[256,1024]{1,0:T(8,128)(2,1)}, u32[]{:S(2)}, u32[]{:S(2)}) collective-permute-start(bf16[256,1024]{1,0:T(8,128)(2,1)} %bitcast.85), channel_id=1, source_target_pairs={{4,0},{8,4},{12,8},{16,12},{20,16},{24,20},{28,24},{32,28},{36,32}... | collective-permute-start | bytes 1572872 | tf_op jit(solution)/shard_map/ppermute | solution.py:13
  14.9 47.0 %collective-permute-start.7 = (bf16[512,1024]{0,1:T(8,128)(2,1)S(1)}, bf16[512,1024]{0,1:T(8,128)(2,1)S(1)}, u32[]{:S(2)}, u32[]{:S(2)}) collective-permute-start(bf16[512,1024]{0,1:T(8,128)(2,1)S(1)} %bitcast.77), channel_id=1, source_target_pairs={{8,0},{12,4},{16,8},{20,12},{24,16},{28,20},{32,24},{36,28},{40,32... | collective-permute-start | bytes 3145736 | tf_op jit(solution)/shard_map/ppermute | solution.py:13
  19.3 30.1 %collective-permute-start.4 = (bf16[512,1024]{0,1:T(8,128)(2,1)S(1)}, bf16[512,1024]{0,1:T(8,128)(2,1)S(1)}, u32[]{:S(2)}, u32[]{:S(2)}) collective-permute-start(bf16[512,1024]{0,1:T(8,128)(2,1)S(1)} %bitcast.78), channel_id=1, source_target_pairs={{504,0},{508,4},{0,8},{4,12},{8,16},{12,20},{16,24},{20,28},{24,32... | collective-permute-start | bytes 3145736 | tf_op jit(solution)/shard_map/ppermute | solution.py:13
  23.7 34.3 %collective-permute-start.5 = (bf16[512,1024]{0,1:T(8,128)(2,1)S(1)}, bf16[512,1024]{0,1:T(8,128)(2,1)S(1)}, u32[]{:S(2)}, u32[]{:S(2)}) collective-permute-start(bf16[512,1024]{0,1:T(8,128)(2,1)S(1)} %bitcast.79), channel_id=1, source_target_pairs={{508,0},{0,4},{4,8},{8,12},{12,16},{16,20},{20,24},{24,28},{28,32}... | collective-permute-start | bytes 3145736 | tf_op jit(solution)/shard_map/ppermute | solution.py:13
  33.2 28.7 %collective-permute-start.6 = (bf16[512,1024]{0,1:T(8,128)(2,1)S(1)}, bf16[512,1024]{0,1:T(8,128)(2,1)S(1)}, u32[]{:S(2)}, u32[]{:S(2)}) collective-permute-start(bf16[512,1024]{0,1:T(8,128)(2,1)S(1)} %bitcast.80), channel_id=1, source_target_pairs={{4,0},{8,4},{12,8},{16,12},{20,16},{24,20},{28,24},{32,28},{36,32}... | collective-permute-start | bytes 3145736 | tf_op jit(solution)/shard_map/ppermute | solution.py:13
  40.3 1.5 copy-start.1
  62.0 2.4 %copy-start = (bf16[5,512,1024]{1,2,0:T(8,128)(2,1)}, bf16[5,512,1024]{1,2,0:T(8,128)(2,1)S(1)}, u32[]{:S(2)}) copy-start(bf16[5,512,1024]{1,2,0:T(8,128)(2,1)S(1)} %bitcast_dynamic-update-slice_fusion) | copy-start | bytes 15728644
where the time goes:
time: 198 us; the launch traced here: 196 us
  local copies, waits for them, and re-layouts  65.1 us (33%)
  matrix products  35.6 us (18%)
  waiting for transfers between devices  27.8 us (14%)
  starting transfers between devices  26.7 us (13%)
  loops' own time  25.2 us (13%)
  blocking collectives  15 us (8%)
    convert_element_type x4, local copies, waits for them, and re-layouts, task_term(): tile = tile.astype(jnp.bfloat16)  45.3 us
    dot_general x4, matrix products, task_term(): lax.dot_general(first, second, (((0,), (0,)), ((), ())), preferred_elemen...  27.9 us
    ppermute x8, waiting for transfers between devices, shifted(): return lax.ppermute(block, axis, route)  27.8 us
    ppermute x8, starting transfers between devices, shifted(): return lax.ppermute(block, axis, route)  26.7 us
    another operation x1, loops' own time, run_tasks(): return lax.fori_loop(first, last, one_task, start)  25.2 us
    all_to_all x1, blocking collectives, summed_on_arrival(): parts = lax.all_to_all(split_up(shard, dim, peers), axis, 0, 0, tiled=True)  15 us
    unnamed x16, local copies, waits for them, and re-layouts  9.57 us
    dot_general x4, matrix products, task_term(): return jnp.dot(amp, tile, preferred_element_type=jnp.float32)  7.68 us
  transfers between devices with their start and end apart: 8, of which 6 were waited for; matrix products, arithmetic and copies ran while one was open for 3% of the time, Pallas kernels for 0%

commit v1 on v0

v1 whole, which is shorter than its diff:
```python
import functools

import jax
import jax.numpy as jnp
from jax import lax
from jax.experimental import pallas as pl
from jax.experimental.pallas import tpu as pltpu
from jax.sharding import PartitionSpec as P

VB = 32
PAIRS = VB * VB
RADIUS = 2
SPAN = 2 * RADIUS + 1
FAR = 3
LANES = 128
GROUPS = LANES // VB
BF16 = jnp.bfloat16
F32 = jnp.float32
ANY = pl.BlockSpec(memory_space=pl.ANY)
SMEM = pl.BlockSpec(memory_space=pltpu.SMEM)
VMEM = pl.BlockSpec(memory_space=pltpu.VMEM)
NT = (((1,), (1,)), ((), ()))


def swap_matrix(dtype):
    row = lax.broadcasted_iota(jnp.int32, (PAIRS, PAIRS), 0)
    col = lax.broadcasted_iota(jnp.int32, (PAIRS, PAIRS), 1)
    hit = row == (col % VB) * VB + col // VB
    return jnp.where(hit, 1.0, 0.0).astype(dtype)


def own_kernel(fac, amp, flipped, amp_out, swap):
    swap[...] = swap_matrix(BF16)
    amp_out[...] = jnp.dot(amp[...], swap[...], preferred_element_type=F32).astype(BF16)
    flipped[...] = lax.dot_general(swap[...], fac[...], NT, preferred_element_type=F32).astype(BF16)


def flip_kernel(fac, flipped, swap):
    swap[...] = swap_matrix(BF16)
    flipped[...] = lax.dot_general(swap[...], fac[...], NT, preferred_element_type=F32).astype(BF16)


def prepare_own(fac, amp):
    quarter = fac.shape[0]
    return pl.pallas_call(
        own_kernel,
        out_shape=(
            jax.ShapeDtypeStruct((PAIRS, quarter), BF16),
            jax.ShapeDtypeStruct(amp.shape, BF16),
        ),
        in_specs=[VMEM, VMEM],
        out_specs=(VMEM, VMEM),
        scratch_shapes=[pltpu.VMEM((PAIRS, PAIRS), BF16)],
        compiler_params=pltpu.CompilerParams(vmem_limit_bytes=24 << 20),
        name="own",
    )(fac, amp)


def flip(fac):
    quarter = fac.shape[0]
    return pl.pallas_call(
        flip_kernel,
        out_shape=jax.ShapeDtypeStruct((PAIRS, quarter), BF16),
        in_specs=[VMEM],
        out_specs=VMEM,
        scratch_shapes=[pltpu.VMEM((PAIRS, PAIRS), BF16)],
        compiler_params=pltpu.CompilerParams(vmem_limit_bytes=24 << 20),
        name="flip",
    )(fac)


def roll_groups(x, groups):
    groups %= GROUPS
    return x if groups == 0 else pltpu.roll(x, groups * VB, 1)


def task_quarter(turned, fac_cols, amp, tile):
    product = jnp.dot(turned, fac_cols, preferred_element_type=F32)
    group = lax.broadcasted_iota(jnp.int32, (VB, LANES), 1) // VB
    for high in range(fac_cols.shape[1] // LANES):
        for d_high in range(VB // GROUPS):
            blocks = []
            for d_low in range(GROUPS):
                first = (d_high * GROUPS + d_low) * VB
                block = product[first : first + VB, high * LANES : (high + 1) * LANES]
                blocks.append(roll_groups(block, d_low))
            for a_low in range(GROUPS):
                mixed = blocks[(0 - a_low) % GROUPS]
                for j in range(1, GROUPS):
                    mixed = jnp.where(group == j, blocks[(j - a_low) % GROUPS], mixed)
                mixed = roll_groups(mixed, -a_low)
                first = (high * GROUPS + a_low) * VB
                tile[first : first + VB, d_high * LANES : (d_high + 1) * LANES] = mixed.astype(BF16)
    return lax.dot_general(amp, tile[...], NT, preferred_element_type=F32)


def start_one(index, sources, target, sem):
    for place, source in sources.items():

        @pl.when(index == place)
        def _():
            pltpu.make_async_copy(source, target, sem).start()


def tasks_kernel(count, plan, *refs, late, places):
    number = len(places)
    facs = dict(zip(places, refs[:number]))
    turned = dict(zip(places, refs[number : 2 * number]))
    amps = dict(enumerate(refs[2 * number : 2 * number + SPAN]))
    rest = refs[2 * number + SPAN :]
    if late:
        before, rest = rest[0], rest[1:]
    out, fac_buf, turn_buf, amp_buf, tile, sems = rest
    slots = plan.shape[0]
    columns = out.shape[2]

    def mine(slot):
        far = jnp.logical_or(plan[slot, 0] == FAR, plan[slot, 1] == FAR)
        return jnp.logical_and(slot < count[0], far if late else jnp.logical_not(far))

    for slot in range(slots):

        @pl.when(mine(slot))
        def _():
            start_one(plan[slot, 1], turned, turn_buf.at[slot], sems.at[slot, 0])
            start_one(plan[slot, 0], facs, fac_buf.at[slot], sems.at[slot, 1])
            start_one(plan[slot, 2], amps, amp_buf.at[slot], sems.at[slot, 2])

    if late:
        out[...] = before[...]
    else:
        out[...] = jnp.zeros_like(out)

    @pl.loop(0, slots)
    def _(slot):
        @pl.when(mine(slot))
        def _():
            pltpu.make_async_copy(turned[0], turn_buf.at[slot], sems.at[slot, 0]).wait()
            pltpu.make_async_copy(facs[0], fac_buf.at[slot], sems.at[slot, 1]).wait()
            pltpu.make_async_copy(amps[0], amp_buf.at[slot], sems.at[slot, 2]).wait()

            @pl.loop(0, out.shape[0])
            def _(part):
                cols = pl.ds(pl.multiple_of(part * columns, columns), columns)
                out[part] += task_quarter(
                    turn_buf[slot], fac_buf[slot, :, cols], amp_buf[slot], tile
                )


def run_tasks(count, plan, facs, turned, amps, before, parts):
    late = before is not None
    places = sorted(facs)
    quarter, occupied = facs[0].shape[0], amps[0].shape[0]
    slots = plan.shape[0]
    columns = PAIRS // parts
    operands = [facs[p] for p in places] + [turned[p] for p in places] + list(amps)
    specs = [ANY] * len(operands)
    if late:
        operands.append(before)
        specs.append(VMEM)
    return pl.pallas_call(
        functools.partial(tasks_kernel, late=late, places=places),
        out_shape=jax.ShapeDtypeStruct((parts, occupied, columns), F32),
        in_specs=[SMEM, SMEM] + specs,
        out_specs=VMEM,
        scratch_shapes=[
            pltpu.VMEM((slots, quarter, PAIRS), BF16),
            pltpu.VMEM((slots, PAIRS, quarter), BF16),
            pltpu.VMEM((slots, occupied, PAIRS), BF16),
            pltpu.VMEM((columns, PAIRS), BF16),
            pltpu.SemaphoreType.DMA((slots, 3)),
        ],
        compiler_params=pltpu.CompilerParams(vmem_limit_bytes=40 << 20),
        name="late" if late else "early",
    )(count, plan, *operands)


def shards(factors, amplitudes, task_counts, task_tiles):
    tiles = lax.axis_size("task")
    parts = lax.axis_size("aux")
    near = [((t + 2 if t % 2 == 0 else t - 2) % tiles, t) for t in range(tiles)]
    far = [((t - 2 if t % 2 == 0 else t + 2) % tiles, t) for t in range(tiles)]
    swap = [(t ^ 1, t) for t in range(tiles)]
    move = lambda x, route: lax.ppermute(x, "task", route)

    fac = factors[0]
    own_turned, own_amp = prepare_own(fac, amplitudes[0])
    sign = 1 - 2 * (lax.axis_index("task") % 2)
    plan = ((task_tiles[0] - RADIUS) * sign) % SPAN

    facs = {0: fac, 1: move(fac, swap), 2: move(fac, near), 3: move(fac, far)}
    facs[4] = move(facs[2], swap)
    amps = {0: own_amp, 1: move(own_amp, swap), 2: move(own_amp, near), 3: move(own_amp, far)}
    amps[4] = move(amps[2], swap)
    amps = [amps[p] for p in range(SPAN)]
    turned = {p: own_turned if p == 0 else flip(facs[p]) for p in range(SPAN)}
    without = lambda d: {p: d[p] for p in d if p != FAR}
    early = run_tasks(task_counts, plan, without(facs), without(turned), amps, None, parts)
    total = run_tasks(task_counts, plan, facs, turned, amps, early, parts)
    mine = lax.axis_index("aux")
    arrived = lax.all_to_all(total.astype(BF16), "aux", 0, 0, tiled=True).astype(F32)
    own = lax.dynamic_index_in_dim(total, mine, 0, False)
    keep = lax.broadcasted_iota(jnp.int32, (parts, 1, 1), 0) == mine
    return jnp.sum(jnp.where(keep, own[None], arrived), axis=0)[None]


def solution(mesh):
    return jax.shard_map(
        shards,
        mesh=mesh,
        in_specs=(P("task", "aux", None), P("task", None, None), P("task"), P("task", None, None)),
        out_specs=P("task", None, "aux"),
        check_vma=False,
    )
```

time: 198 us -> 104 us (0.53)
  the two profiles are of different devices: /device:TPU:448 before, /device:TPU:2 now
where the time goes in v1:
time: 104 us; the launch traced here: 103 us
  starting transfers between devices  39.6 us (38%)
  Pallas kernels  31.4 us (30%)
  waiting for transfers between devices  22.4 us (22%)
  local copies, waits for them, and re-layouts  6.94 us (7%)
  other arithmetic  1.78 us (2%)
    ppermute x8, starting transfers between devices, shards(): move = lambda x, route: lax.ppermute(x, 'task', route)  34.8 us
    pallas_call x2, Pallas kernels, run_tasks(): pl.pallas_call(functools.partial(tasks_kernel, late=late, places=places),...  23.2 us
    ppermute x8, waiting for transfers between devices, shards(): move = lambda x, route: lax.ppermute(x, 'task', route)  16.7 us
    pallas_call x4, Pallas kernels, flip(): pl.pallas_call(flip_kernel, out_shape=jax.ShapeDtypeStruct((PAIRS, quarte...  6.35 us
    unnamed x16, local copies, waits for them, and re-layouts  5.88 us
    all_to_all x1, waiting for transfers between devices, shards(): lax.all_to_all(total.astype(BF16), 'aux', 0, 0, tiled=True).astype(F32)  5.65 us
    all_to_all x1, starting transfers between devices, shards(): lax.all_to_all(total.astype(BF16), 'aux', 0, 0, tiled=True).astype(F32)  4.82 us
  transfers between devices with their start and end apart: 9, of which 4 were waited for; matrix products, arithmetic and copies ran while one was open for 1% of the time, Pallas kernels for 8%

profile of v1, /device:TPU:2, one launch (start us, length us, event | category | flops | bytes accessed | tf_op | source)
XLA Modules:
  0.0 103.0 jit_solution(11928598734636618602)
XLA Ops:
  0.0 13.8 %collective-permute-start.1 = (bf16[512,1024]{1,0:T(8,128)(2,1)}, bf16[512,1024]{1,0:T(8,128)(2,1)S(1)}, u32[]{:S(2)}, u32[]{:S(2)}) collective-permute-start(bf16[512,1024]{1,0:T(8,128)(2,1)} %bitcast.15), channel_id=1, source_target_pairs={{8,0},{508,4},{16,8},{4,12},{24,16},{12,20},{32,24},{20,28},{40,32... | collective-permute-start | bytes 3145736 | tf_op jit(solution)/shard_map/ppermute | solution.py:184
  13.9 1.9 %collective-permute-start = (bf16[512,1024]{1,0:T(8,128)(2,1)}, bf16[512,1024]{1,0:T(8,128)(2,1)S(1)}, u32[]{:S(2)}, u32[]{:S(2)}) collective-permute-start(bf16[512,1024]{1,0:T(8,128)(2,1)} %bitcast.16), channel_id=1, source_target_pairs={{4,0},{0,4},{12,8},{8,12},{20,16},{16,20},{28,24},{24,28},{36,32},... | collective-permute-start | bytes 3145736 | tf_op jit(solution)/shard_map/ppermute | solution.py:184
  15.8 1.9 %collective-permute-start.2 = (bf16[512,1024]{1,0:T(8,128)(2,1)}, bf16[512,1024]{1,0:T(8,128)(2,1)}, u32[]{:S(2)}, u32[]{:S(2)}) collective-permute-start(bf16[512,1024]{1,0:T(8,128)(2,1)} %bitcast.17), channel_id=1, source_target_pairs={{504,0},{12,4},{0,8},{20,12},{8,16},{28,20},{16,24},{36,28},{24,32... | collective-permute-start | bytes 3145736 | tf_op jit(solution)/shard_map/ppermute | solution.py:184
  17.7 0.0 copy-start
  17.7 1.2 %copy-done = bf16[1,512,1024]{2,1,0:T(8,128)(2,1)S(1)} copy-done((bf16[1,512,1024]{2,1,0:T(8,128)(2,1)S(1)}, bf16[1,512,1024]{2,1,0:T(8,128)(2,1)}, u32[]{:S(2)}) %copy-start) | copy-done | bytes 1048600
  19.0 1.0 %copy-done.6 = bf16[1,256,1024]{2,1,0:T(8,128)(2,1)S(1)} copy-done((bf16[1,256,1024]{2,1,0:T(8,128)(2,1)S(1)}, bf16[1,256,1024]{2,1,0:T(8,128)(2,1)}, u32[]{:S(2)}) %copy-start.6) | copy-done | bytes 524312
  20.0 1.9 %own.1 = (bf16[1024,512]{1,0:T(8,128)(2,1)S(1)}, bf16[256,1024]{1,0:T(8,128)(2,1)}) custom-call(bf16[512,1024]{1,0:T(8,128)(2,1)S(1)} %bitcast.18, bf16[256,1024]{1,0:T(8,128)(2,1)S(1)} %bitcast.21), custom_call_target="tpu_custom_call" | custom-call | tf_op jit(solution)/shard_map/own/pallas_call | solution.py:45
  21.9 1.0 copy-done.3
  22.9 10.0 %collective-permute-done.1.fac.refs_2_ = bf16[512,1024]{1,0:T(8,128)(2,1)S(1)} collective-permute-done((bf16[512,1024]{1,0:T(8,128)(2,1)}, bf16[512,1024]{1,0:T(8,128)(2,1)S(1)}, u32[]{:S(2)}, u32[]{:S(2)}) %collective-permute-start.1) | collective-permute-done | bytes 1048608 | tf_op jit(solution)/shard_map/ppermute | solution.py:184
  32.9 1.9 %collective-permute-start.3 = (bf16[512,1024]{1,0:T(8,128)(2,1)S(1)}, bf16[512,1024]{1,0:T(8,128)(2,1)S(1)}, u32[]{:S(2)}, u32[]{:S(2)}) collective-permute-start(bf16[512,1024]{1,0:T(8,128)(2,1)S(1)} %collective-permute-done.1.fac.refs_2_), channel_id=1, source_target_pairs={{4,0},{0,4},{12,8},{8,12},{20,16},{16,20},{28,24},{24,28},{36,32},... | collective-permute-start | bytes 3145736 | tf_op jit(solution)/shard_map/ppermute | solution.py:184
  34.8 7.6 %collective-permute-start.5 = (bf16[256,1024]{1,0:T(8,128)(2,1)}, bf16[256,1024]{1,0:T(8,128)(2,1)}, u32[]{:S(2)}, u32[]{:S(2)}) collective-permute-start(bf16[256,1024]{1,0:T(8,128)(2,1)} %get-tuple-element.8.refs_8_.refs_10_), channel_id=1, source_target_pairs={{8,0},{508,4},{16,8},{4,12},{24,16},{12,20},{32,24},{20,28},{40,32... | collective-permute-start | bytes 1572872 | tf_op jit(solution)/shard_map/ppermute | solution.py:184
  42.4 1.9 %collective-permute-start.4 = (bf16[256,1024]{1,0:T(8,128)(2,1)}, bf16[256,1024]{1,0:T(8,128)(2,1)}, u32[]{:S(2)}, u32[]{:S(2)}) collective-permute-start(bf16[256,1024]{1,0:T(8,128)(2,1)} %get-tuple-element.8.refs_8_.refs_10_), channel_id=1, source_target_pairs={{4,0},{0,4},{12,8},{8,12},{20,16},{16,20},{28,24},{24,28},{36,32},... | collective-permute-start | bytes 1572872 | tf_op jit(solution)/shard_map/ppermute | solution.py:184
  44.4 5.1 %collective-permute-done.5.refs_10_.refs_12_ = bf16[256,1024]{1,0:T(8,128)(2,1)} collective-permute-done((bf16[256,1024]{1,0:T(8,128)(2,1)}, bf16[256,1024]{1,0:T(8,128)(2,1)}, u32[]{:S(2)}, u32[]{:S(2)}) %collective-permute-start.5) | collective-permute-done | bytes 524320 | tf_op jit(solution)/shard_map/ppermute | solution.py:184
  49.4 1.9 %collective-permute-start.6 = (bf16[256,1024]{1,0:T(8,128)(2,1)}, bf16[256,1024]{1,0:T(8,128)(2,1)}, u32[]{:S(2)}, u32[]{:S(2)}) collective-permute-start(bf16[256,1024]{1,0:T(8,128)(2,1)} %get-tuple-element.8.refs_8_.refs_10_), channel_id=1, source_target_pairs={{504,0},{12,4},{0,8},{20,12},{8,16},{28,20},{16,24},{36,28},{24,32... | collective-permute-start | bytes 1572872 | tf_op jit(solution)/shard_map/ppermute | solution.py:184
  51.4 3.7 %collective-permute-start.7 = (bf16[256,1024]{1,0:T(8,128)(2,1)}, bf16[256,1024]{1,0:T(8,128)(2,1)}, u32[]{:S(2)}, u32[]{:S(2)}) collective-permute-start(bf16[256,1024]{1,0:T(8,128)(2,1)} %collective-permute-done.5.refs_10_.refs_12_), channel_id=1, source_target_pairs={{4,0},{0,4},{12,8},{8,12},{20,16},{16,20},{28,24},{24,28},{36,32},... | collective-permute-start | bytes 1572872 | tf_op jit(solution)/shard_map/ppermute | solution.py:184
  55.1 0.0 copy-start.7
  55.1 0.7 copy-done.7
  55.8 0.1 copy.5
  56.6 1.3 %flip.5.refs_6_.refs_7_ = bf16[1024,512]{1,0:T(8,128)(2,1)S(1)} custom-call(bf16[512,1024]{1,0:T(8,128)(2,1)S(1)} %collective-permute-done.1.fac.refs_2_), custom_call_target="tpu_custom_call" | custom-call | tf_op jit(solution)/shard_map/flip/pallas_call | solution.py:61
  57.9 1.3 %flip.4.refs_5_.refs_6_ = bf16[1024,512]{1,0:T(8,128)(2,1)S(1)} custom-call(bf16[512,1024]{1,0:T(8,128)(2,1)S(1)} %collective-permute-done.fac.refs_1_), custom_call_target="tpu_custom_call" | custom-call | tf_op jit(solution)/shard_map/flip/pallas_call | solution.py:61
  59.2 2.5 %flip.6.refs_8_ = bf16[1024,512]{1,0:T(8,128)(2,1)S(1)} custom-call(bf16[512,1024]{1,0:T(8,128)(2,1)} %collective-permute-done.2.fac.refs_3_), custom_call_target="tpu_custom_call" | custom-call | tf_op jit(solution)/shard_map/flip/pallas_call | solution.py:61
  61.7 1.3 %flip.7.refs_7_.refs_9_ = bf16[1024,512]{1,0:T(8,128)(2,1)S(1)} custom-call(bf16[512,1024]{1,0:T(8,128)(2,1)S(1)} %collective-permute-done.3.fac.refs_3_.refs_4_), custom_call_target="tpu_custom_call" | custom-call | tf_op jit(solution)/shard_map/flip/pallas_call | solution.py:61
  63.0 1.6 %collective-permute-done.6.refs_11_.refs_13_ = bf16[256,1024]{1,0:T(8,128)(2,1)} collective-permute-done((bf16[256,1024]{1,0:T(8,128)(2,1)}, bf16[256,1024]{1,0:T(8,128)(2,1)}, u32[]{:S(2)}, u32[]{:S(2)}) %collective-permute-start.6) | collective-permute-done | bytes 524320 | tf_op jit(solution)/shard_map/ppermute | solution.py:184
  64.6 11.3 %early.1.refs_15_ = f32[4,256,256]{2,1,0:T(8,128)S(1)} custom-call(s32[1]{0:T(128)S(6)} %copy.6.count, s32[4,3]{1,0:T(4,128)S(1)} %add_select_fusion.plan, bf16[512,1024]{1,0:T(8,128)(2,1)S(1)} %bitcast.19, bf16[512,1024]{1,0:T(8,128)(2,1)S(1)} %collective-permute-done.fac.refs_1_, bf16[512,1024]{1,0:T(8,128)(2,1)S(1)} %collective-permute-done.1.fac.refs_2_, ...), custom_call_target="tpu_custom_call" | custom-call | tf_op jit(solution)/shard_map/early/pallas_call | solution.py:161
  75.9 1.0 copy-done.5
  76.9 12.0 %late.1 = f32[4,256,256]{2,1,0:T(8,128)S(1)} custom-call(s32[1]{0:T(128)S(6)} %copy.6.count, s32[4,3]{1,0:T(4,128)S(1)} %add_select_fusion.plan, bf16[512,1024]{1,0:T(8,128)(2,1)S(1)} %bitcast.20, bf16[512,1024]{1,0:T(8,128)(2,1)S(1)} %collective-permute-done.fac.refs_1_, bf16[512,1024]{1,0:T(8,128)(2,1)S(1)} %collective-permute-done.1.fac.refs_2_, ...), custom_call_target="tpu_custom_call" | custom-call | tf_op jit(solution)/shard_map/late/pallas_call | solution.py:161
  88.9 1.0 copy-done.2
  89.8 0.9 convert_element_type.6
  90.7 4.8 %all-to-all-start = ((bf16[4,256,256]{2,1,0:T(8,128)(2,1)}), bf16[4,256,256]{2,1,0:T(8,128)(2,1)S(1)}, u32[]{:S(2)}, u32[]{:S(2)}) async-start(bf16[4,256,256]{2,1,0:T(8,128)(2,1)} %convert_element_type.6), calls=%async_computation | async-start | bytes 1048576 | tf_op jit(solution)/shard_map/all_to_all | solution.py:201
  95.5 1.0 dynamic-slice_bitcast_fusion
  96.5 5.6 %all-to-all-done = bf16[4,256,256]{2,1,0:T(8,128)(2,1)S(1)} async-done(((bf16[4,256,256]{2,1,0:T(8,128)(2,1)}), bf16[4,256,256]{2,1,0:T(8,128)(2,1)S(1)}, u32[]{:S(2)}, u32[]{:S(2)}) %all-to-all-start) | async-done | bytes 524320 | tf_op jit(solution)/shard_map/all_to_all | solution.py:201
  102.1 0.9 select_reduce_fusion
  (16 shorter events, 0.1 us)
Async XLA Ops:
  0.0 32.9 %collective-permute-start.1 = (bf16[512,1024]{1,0:T(8,128)(2,1)}, bf16[512,1024]{1,0:T(8,128)(2,1)S(1)}, u32[]{:S(2)}, u32[]{:S(2)}) collective-permute-start(bf16[512,1024]{1,0:T(8,128)(2,1)} %bitcast.15), channel_id=1, source_target_pairs={{8,0},{508,4},{16,8},{4,12},{24,16},{12,20},{32,24},{20,28},{40,32... | collective-permute-start | bytes 3145736 | tf_op jit(solution)/shard_map/ppermute | solution.py:184
  13.9 37.5 %collective-permute-start = (bf16[512,1024]{1,0:T(8,128)(2,1)}, bf16[512,1024]{1,0:T(8,128)(2,1)S(1)}, u32[]{:S(2)}, u32[]{:S(2)}) collective-permute-start(bf16[512,1024]{1,0:T(8,128)(2,1)} %bitcast.16), channel_id=1, source_target_pairs={{4,0},{0,4},{12,8},{8,12},{20,16},{16,20},{28,24},{24,28},{36,32},... | collective-permute-start | bytes 3145736 | tf_op jit(solution)/shard_map/ppermute | solution.py:184
  15.8 43.4 %collective-permute-start.2 = (bf16[512,1024]{1,0:T(8,128)(2,1)}, bf16[512,1024]{1,0:T(8,128)(2,1)}, u32[]{:S(2)}, u32[]{:S(2)}) collective-permute-start(bf16[512,1024]{1,0:T(8,128)(2,1)} %bitcast.17), channel_id=1, source_target_pairs={{504,0},{12,4},{0,8},{20,12},{8,16},{28,20},{16,24},{36,28},{24,32... | collective-permute-start | bytes 3145736 | tf_op jit(solution)/shard_map/ppermute | solution.py:184
  17.7 1.2 %copy-start = (bf16[1,512,1024]{2,1,0:T(8,128)(2,1)S(1)}, bf16[1,512,1024]{2,1,0:T(8,128)(2,1)}, u32[]{:S(2)}) copy-start(bf16[1,512,1024]{2,1,0:T(8,128)(2,1)} %param.4) | copy-start | bytes 3145732
  19.0 1.0 %copy-start.6 = (bf16[1,256,1024]{2,1,0:T(8,128)(2,1)S(1)}, bf16[1,256,1024]{2,1,0:T(8,128)(2,1)}, u32[]{:S(2)}) copy-start(bf16[1,256,1024]{2,1,0:T(8,128)(2,1)} %param.5) | copy-start | bytes 1572868
  21.9 1.0 copy-start.3
  32.9 28.8 %collective-permute-start.3 = (bf16[512,1024]{1,0:T(8,128)(2,1)S(1)}, bf16[512,1024]{1,0:T(8,128)(2,1)S(1)}, u32[]{:S(2)}, u32[]{:S(2)}) collective-permute-start(bf16[512,1024]{1,0:T(8,128)(2,1)S(1)} %collective-permute-done.1.fac.refs_2_), channel_id=1, source_target_pairs={{4,0},{0,4},{12,8},{8,12},{20,16},{16,20},{28,24},{24,28},{36,32},... | collective-permute-start | bytes 3145736 | tf_op jit(solution)/shard_map/ppermute | solution.py:184
  34.8 14.6 %collective-permute-start.5 = (bf16[256,1024]{1,0:T(8,128)(2,1)}, bf16[256,1024]{1,0:T(8,128)(2,1)}, u32[]{:S(2)}, u32[]{:S(2)}) collective-permute-start(bf16[256,1024]{1,0:T(8,128)(2,1)} %get-tuple-element.8.refs_8_.refs_10_), channel_id=1, source_target_pairs={{8,0},{508,4},{16,8},{4,12},{24,16},{12,20},{32,24},{20,28},{40,32... | collective-permute-start | bytes 1572872 | tf_op jit(solution)/shard_map/ppermute | solution.py:184
  42.4 20.6 %collective-permute-start.4 = (bf16[256,1024]{1,0:T(8,128)(2,1)}, bf16[256,1024]{1,0:T(8,128)(2,1)}, u32[]{:S(2)}, u32[]{:S(2)}) collective-permute-start(bf16[256,1024]{1,0:T(8,128)(2,1)} %get-tuple-element.8.refs_8_.refs_10_), channel_id=1, source_target_pairs={{4,0},{0,4},{12,8},{8,12},{20,16},{16,20},{28,24},{24,28},{36,32},... | collective-permute-start | bytes 1572872 | tf_op jit(solution)/shard_map/ppermute | solution.py:184
  49.4 15.2 %collective-permute-start.6 = (bf16[256,1024]{1,0:T(8,128)(2,1)}, bf16[256,1024]{1,0:T(8,128)(2,1)}, u32[]{:S(2)}, u32[]{:S(2)}) collective-permute-start(bf16[256,1024]{1,0:T(8,128)(2,1)} %get-tuple-element.8.refs_8_.refs_10_), channel_id=1, source_target_pairs={{504,0},{12,4},{0,8},{20,12},{8,16},{28,20},{16,24},{36,28},{24,32... | collective-permute-start | bytes 1572872 | tf_op jit(solution)/shard_map/ppermute | solution.py:184
  51.4 13.2 %collective-permute-start.7 = (bf16[256,1024]{1,0:T(8,128)(2,1)}, bf16[256,1024]{1,0:T(8,128)(2,1)}, u32[]{:S(2)}, u32[]{:S(2)}) collective-permute-start(bf16[256,1024]{1,0:T(8,128)(2,1)} %collective-permute-done.5.refs_10_.refs_12_), channel_id=1, source_target_pairs={{4,0},{0,4},{12,8},{8,12},{20,16},{16,20},{28,24},{24,28},{36,32},... | collective-permute-start | bytes 1572872 | tf_op jit(solution)/shard_map/ppermute | solution.py:184
  55.1 0.7 copy-start.7
  61.7 2.9 %copy-start.1 = (bf16[1,512,1024]{2,1,0:T(8,128)(2,1)S(1)}, bf16[1,512,1024]{2,1,0:T(8,128)(2,1)}, u32[]{:S(2)}) copy-start(bf16[1,512,1024]{2,1,0:T(8,128)(2,1)} %param.4) | copy-start | bytes 3145732
  61.7 2.9 %copy-start.4 = (bf16[1024,512]{1,0:T(8,128)(2,1)S(1)}, bf16[1024,512]{1,0:T(8,128)(2,1)}, u32[]{:S(2)}) copy-start(bf16[1024,512]{1,0:T(8,128)(2,1)} %copy-done.3) | copy-start | bytes 3145732
  75.9 1.0 copy-start.5
  88.8 1.0 copy-start.2
  90.7 11.4 %all-to-all-start = ((bf16[4,256,256]{2,1,0:T(8,128)(2,1)}), bf16[4,256,256]{2,1,0:T(8,128)(2,1)S(1)}, u32[]{:S(2)}, u32[]{:S(2)}) async-start(bf16[4,256,256]{2,1,0:T(8,128)(2,1)} %convert_element_type.6), calls=%async_computation | async-start | bytes 1048576 | tf_op jit(solution)/shard_map/all_to_all | solution.py:201

commit v2 on v1

v2 whole, which is shorter than its diff:
```python
import functools

import jax
import jax.numpy as jnp
from jax import lax
from jax.experimental import pallas as pl
from jax.experimental.pallas import tpu as pltpu
from jax.sharding import PartitionSpec as P

VB = 32
PAIRS = VB * VB
RADIUS = 2
SPAN = 2 * RADIUS + 1
FAR = 3
LANES = 128
GROUPS = LANES // VB
BF16 = jnp.bfloat16
F32 = jnp.float32
HBM = pl.BlockSpec(memory_space=pltpu.HBM)
SMEM = pl.BlockSpec(memory_space=pltpu.SMEM)
VMEM = pl.BlockSpec(memory_space=pltpu.VMEM)
NT = (((1,), (1,)), ((), ()))


def swap_matrix():
    row = lax.broadcasted_iota(jnp.int32, (PAIRS, PAIRS), 0)
    col = lax.broadcasted_iota(jnp.int32, (PAIRS, PAIRS), 1)
    hit = row == (col % VB) * VB + col // VB
    return jnp.where(hit, 1.0, 0.0).astype(BF16)


def params(mib):
    return pltpu.CompilerParams(vmem_limit_bytes=mib << 20)


def cost(flops, moved):
    return pl.CostEstimate(flops=flops, bytes_accessed=moved, transcendentals=0)


def pack_kernel(fac, amp, out, amp_out, swap, fac_buf, sems):
    depth = fac.shape[0]
    arrive = pltpu.make_async_copy(fac, fac_buf, sems.at[0])
    arrive.start()
    swap[...] = swap_matrix()
    arrive.wait()
    leave = pltpu.make_async_copy(fac_buf, out.at[:depth], sems.at[1])
    leave.start()
    amp_out[...] = jnp.dot(amp[...], swap[...], preferred_element_type=F32).astype(BF16)
    other = pltpu.make_async_copy(amp_out, out.at[depth:], sems.at[2])
    other.start()
    leave.wait()
    other.wait()


def pack(fac, amp):
    return pl.pallas_call(
        pack_kernel,
        out_shape=(
            jax.ShapeDtypeStruct((fac.shape[0] + amp.shape[0], PAIRS), BF16),
            jax.ShapeDtypeStruct(amp.shape, BF16),
        ),
        in_specs=[HBM, VMEM],
        out_specs=(HBM, VMEM),
        scratch_shapes=[
            pltpu.VMEM((PAIRS, PAIRS), BF16),
            pltpu.VMEM(fac.shape, BF16),
            pltpu.SemaphoreType.DMA((3,)),
        ],
        compiler_params=params(34),
        cost_estimate=cost(1, 1),
        name="pack",
    )(fac, amp)


def roll_groups(x, groups):
    groups %= GROUPS
    return x if groups == 0 else pltpu.roll(x, groups * VB, 1)


def write_tile(product, tile):
    group = lax.broadcasted_iota(jnp.int32, (VB, LANES), 1) // VB
    for high in range(PAIRS // LANES):
        for d_high in range(VB // GROUPS):
            blocks = []
            for d_low in range(GROUPS):
                first = (d_high * GROUPS + d_low) * VB
                block = product[first : first + VB, high * LANES : (high + 1) * LANES]
                blocks.append(roll_groups(block, d_low))
            for a_low in range(GROUPS):
                mixed = blocks[(0 - a_low) % GROUPS]
                for j in range(1, GROUPS):
                    mixed = jnp.where(group == j, blocks[(j - a_low) % GROUPS], mixed)
                first = high * LANES + a_low * VB
                tile[first : first + VB, d_high * LANES : (d_high + 1) * LANES] = roll_groups(
                    mixed, -a_low
                )


def start_one(index, sources, target, sem):
    for place, source in sources.items():

        @pl.when(index == place)
        def _():
            pltpu.make_async_copy(source, target, sem).start()


EMPTY, READY, FIRST, SECOND = range(4)


def slot_table(count, plan):
    sign = 1 - 2 * (lax.axis_index("task") % 2)
    distance = (plan - RADIUS) * sign
    places = jnp.where(distance < 0, distance + SPAN, distance)
    kind = jnp.where(places[:, 0] == FAR, FIRST, READY)
    kind = jnp.where(places[:, 1] == FAR, SECOND, kind)
    kind = jnp.where(jnp.arange(plan.shape[0]) < count[0], kind, EMPTY)
    return jnp.concatenate([kind[:, None], places], axis=1).astype(jnp.int32)


def any_slot(hits, slots):
    return functools.reduce(jnp.logical_or, [hits(slot) for slot in range(slots)])


def turn(swap, fac):
    return lax.dot_general(swap[...], fac, NT, preferred_element_type=F32).astype(BF16)


def early_kernel(table, own, partner, near, partner_near, out, turned_out, *scratch):
    left, right, turned, swap, tiles, sems = scratch
    depth, slots = near.shape[0], table.shape[0]
    facs = {0: own.at[:depth], 1: partner.at[:depth], 2: near, 4: partner_near}
    whole = lambda s: table[s, 0] == READY
    half = lambda s: table[s, 0] == FIRST
    mine = lambda s: jnp.logical_or(whole(s), half(s))
    tile_copy = lambda s: pltpu.make_async_copy(tiles.at[s], out.at[s], sems.at[s, 2])
    turned_copy = lambda s: pltpu.make_async_copy(turned.at[s], turned_out.at[s], sems.at[s, 3])
    for slot in range(slots):

        @pl.when(mine(slot))
        def _():
            start_one(table[slot, 2], facs, right.at[slot], sems.at[slot, 1])

        @pl.when(whole(slot))
        def _():
            start_one(table[slot, 1], facs, left.at[slot], sems.at[slot, 0])

    @pl.when(any_slot(mine, slots))
    def _():
        swap[...] = swap_matrix()

    @pl.loop(0, slots)
    def _(slot):
        @pl.when(mine(slot))
        def _():
            pltpu.make_async_copy(near, right.at[slot], sems.at[slot, 1]).wait()
            turned[slot] = turn(swap, right[slot])

        @pl.when(half(slot))
        def _():
            turned_copy(slot).start()

        @pl.when(whole(slot))
        def _():
            pltpu.make_async_copy(near, left.at[slot], sems.at[slot, 0]).wait()
            product = jnp.dot(turned[slot], left[slot], preferred_element_type=F32)
            write_tile(product.astype(BF16), tiles.at[slot])
            tile_copy(slot).start()

    for slot in range(slots):
        pl.when(whole(slot))(lambda: tile_copy(slot).wait())
        pl.when(half(slot))(lambda: turned_copy(slot).wait())


def turn_kernel(table, far, out, swap, fac, turned, sems):
    slots = table.shape[0]

    @pl.when(any_slot(lambda s: table[s, 0] == SECOND, slots))
    def _():
        arrive = pltpu.make_async_copy(far.at[: fac.shape[0]], fac, sems.at[0])
        arrive.start()
        swap[...] = swap_matrix()
        arrive.wait()
        turned[...] = turn(swap, fac[...])
        leave = pltpu.make_async_copy(turned, out, sems.at[1])
        leave.start()
        leave.wait()


def late_kernel(
    table, early, early_turned, far_turned, own, partner, near, partner_near, far, amp_2, amp_4, *refs
):
    sent, kept, total, amp_buf, left, turned, tiles, sems = refs
    depth, slots = near.shape[0], table.shape[0]
    facs = {0: own.at[:depth], 1: partner.at[:depth], 2: near, 3: far.at[:depth], 4: partner_near}
    amps = {0: own.at[depth:], 1: partner.at[depth:], 2: amp_2, 3: far.at[depth:], 4: amp_4}
    live = lambda s: table[s, 0] != EMPTY
    mine = lambda s: table[s, 0] >= FIRST
    made = lambda s: table[s, 0] == READY
    for slot in range(slots):

        @pl.when(mine(slot))
        def _():
            right_far = table[slot, 0] == SECOND

            @pl.when(right_far)
            def _():
                pltpu.make_async_copy(far_turned, turned.at[slot], sems.at[slot, 1]).start()

            @pl.when(jnp.logical_not(right_far))
            def _():
                pltpu.make_async_copy(early_turned.at[slot], turned.at[slot], sems.at[slot, 1]).start()

            start_one(table[slot, 1], facs, left.at[slot], sems.at[slot, 0])

        @pl.when(made(slot))
        def _():
            pltpu.make_async_copy(early.at[slot], tiles.at[slot], sems.at[slot, 2]).start()

        @pl.when(live(slot))
        def _():
            start_one(table[slot, 3], amps, amp_buf.at[slot], sems.at[slot, 3])

    total[...] = jnp.zeros_like(total)

    @pl.loop(0, slots)
    def _(slot):
        @pl.when(mine(slot))
        def _():
            pltpu.make_async_copy(far_turned, turned.at[slot], sems.at[slot, 1]).wait()
            pltpu.make_async_copy(near, left.at[slot], sems.at[slot, 0]).wait()
            product = jnp.dot(turned[slot], left[slot], preferred_element_type=F32)
            write_tile(product.astype(BF16), tiles.at[slot])

        @pl.when(made(slot))
        def _():
            pltpu.make_async_copy(early.at[slot], tiles.at[slot], sems.at[slot, 2]).wait()

        @pl.when(live(slot))
        def _():
            pltpu.make_async_copy(amp_2, amp_buf.at[slot], sems.at[slot, 3]).wait()
            total[...] += lax.dot_general(
                amp_buf[slot], tiles[slot], NT, preferred_element_type=F32
            )

    place = lax.axis_index("aux")
    columns = kept.shape[1]
    for part in range(sent.shape[0]):
        values = total[:, part * columns : (part + 1) * columns]
        sent[part] = jnp.where(place == part, 0.0, values).astype(BF16)
    kept[...] = total[:, pl.ds(pl.multiple_of(place * columns, columns), columns)]


def early_tiles(table, own, partner, near, partner_near):
    slots, quarter = table.shape[0], near.shape[0]
    return pl.pallas_call(
        early_kernel,
        out_shape=(
            jax.ShapeDtypeStruct((slots, PAIRS, PAIRS), BF16),
            jax.ShapeDtypeStruct((slots, PAIRS, quarter), BF16),
        ),
        in_specs=[SMEM] + [HBM] * 4,
        out_specs=(HBM, HBM),
        scratch_shapes=[
            pltpu.VMEM((slots, quarter, PAIRS), BF16),
            pltpu.VMEM((slots, quarter, PAIRS), BF16),
            pltpu.VMEM((slots, PAIRS, quarter), BF16),
            pltpu.VMEM((PAIRS, PAIRS), BF16),
            pltpu.VMEM((slots, PAIRS, PAIRS), BF16),
            pltpu.SemaphoreType.DMA((slots, 4)),
        ],
        compiler_params=params(34),
        cost_estimate=cost(1, 1),
        name="early",
    )(table, own, partner, near, partner_near)


def turn_far(table, far, quarter):
    return pl.pallas_call(
        turn_kernel,
        out_shape=jax.ShapeDtypeStruct((PAIRS, quarter), BF16),
        in_specs=[SMEM, HBM],
        out_specs=HBM,
        scratch_shapes=[
            pltpu.VMEM((PAIRS, PAIRS), BF16),
            pltpu.VMEM((quarter, PAIRS), BF16),
            pltpu.VMEM((PAIRS, quarter), BF16),
            pltpu.SemaphoreType.DMA((2,)),
        ],
        compiler_params=params(34),
        cost_estimate=cost(20 * quarter * PAIRS * PAIRS, 1 << 20),
        name="turn",
    )(table, far)


def all_terms(table, early, early_turned, far_turned, own, partner, near, partner_near, far, amp_2, amp_4, parts):
    slots, columns, occupied, quarter = table.shape[0], PAIRS // parts, amp_2.shape[0], near.shape[0]
    return pl.pallas_call(
        late_kernel,
        out_shape=(
            jax.ShapeDtypeStruct((parts, occupied, columns), BF16),
            jax.ShapeDtypeStruct((occupied, columns), F32),
        ),
        in_specs=[SMEM] + [HBM] * 10,
        out_specs=(VMEM, VMEM),
        scratch_shapes=[
            pltpu.VMEM((occupied, PAIRS), F32),
            pltpu.VMEM((slots, occupied, PAIRS), BF16),
            pltpu.VMEM((slots, quarter, PAIRS), BF16),
            pltpu.VMEM((slots, PAIRS, quarter), BF16),
            pltpu.VMEM((slots, PAIRS, PAIRS), BF16),
            pltpu.SemaphoreType.DMA((slots, 4)),
        ],
        compiler_params=params(34),
        cost_estimate=cost(1, 1),
        name="late",
    )(table, early, early_turned, far_turned, own, partner, near, partner_near, far, amp_2, amp_4)


def after(x, *others):
    return lax.optimization_barrier((x, *others))[0]


def shards(factors, amplitudes, task_counts, task_tiles):
    tiles = lax.axis_size("task")
    parts = lax.axis_size("aux")
    near = [((t + 2 if t % 2 == 0 else t - 2) % tiles, t) for t in range(tiles)]
    far = [((t - 2 if t % 2 == 0 else t + 2) % tiles, t) for t in range(tiles)]
    swap = [(t ^ 1, t) for t in range(tiles)]
    move = lambda x, route: lax.ppermute(x, "task", route)

    fac = factors[0]
    table = slot_table(task_counts, task_tiles[0])
    fac_2 = move(fac, near)
    own, amp = pack(fac, amplitudes[0])
    packed_3 = move(own, far)
    packed_1 = move(own, swap)
    amp_2 = move(amp, near)
    fac_4 = move(fac_2, swap)
    early, early_turned = early_tiles(table, own, packed_1, fac_2, fac_4)
    amp_4 = move(after(amp_2, early), swap)
    far_turned = turn_far(table, packed_3, fac.shape[0])
    sent, kept = all_terms(
        table,
        early,
        early_turned,
        far_turned,
        own,
        packed_1,
        fac_2,
        fac_4,
        packed_3,
        amp_2,
        amp_4,
        parts,
    )
    arrived = lax.all_to_all(sent, "aux", 0, 0, tiled=True)
    return (kept + jnp.sum(arrived.astype(F32), axis=0))[None]


def solution(mesh):
    return jax.shard_map(
        shards,
        mesh=mesh,
        in_specs=(P("task", "aux", None), P("task", None, None), P("task"), P("task", None, None)),
        out_specs=P("task", None, "aux"),
        check_vma=False,
    )
```

time: 104 us -> 74.5 us (0.72)
  waiting for transfers between devices: 22.4 us -> 8.41 us
  Pallas kernels: 31.4 us -> 17.9 us
  blocking collectives: 0 us -> 11.7 us
  starting transfers between devices: 39.6 us -> 31.8 us
  local copies, waits for them, and re-layouts: 6.94 us -> 2.37 us
    pallas_call x7 -> x4, Pallas kernels: 31.4 us -> 17.9 us  [the longest x1 8.95 us: early_tiles(): pl.pallas_call(early_kernel, out_shape=(jax.ShapeDtypeStruct((slots, PAIR...]
    all_to_all x0 -> x1, blocking collectives: none -> 11.7 us  [shards(): arrived = lax.all_to_all(sent, 'aux', 0, 0, tiled=True)]
    ppermute x8 -> x6, waiting for transfers between devices: 16.7 us -> 8.41 us  [shards(): move = lambda x, route: lax.ppermute(x, 'task', route)]
    all_to_all x1 -> x0, waiting for transfers between devices: 5.65 us -> none  [shards(): lax.all_to_all(total.astype(BF16), 'aux', 0, 0, tiled=True).astype(F32)]
    all_to_all x1 -> x0, starting transfers between devices: 4.82 us -> none  [shards(): lax.all_to_all(total.astype(BF16), 'aux', 0, 0, tiled=True).astype(F32)]
    unnamed x16 -> x8, local copies, waits for them, and re-layouts: 5.88 us -> 2.28 us
    ppermute x8 -> x6, starting transfers between devices: 34.8 us -> 31.8 us  [shards(): move = lambda x, route: lax.ppermute(x, 'task', route)]
  transfers between devices with their start and end apart: 9 -> 6, of which waited for: 4 -> 3; matrix products, arithmetic and copies ran while one was open for 1% -> 0% of each run, Pallas kernels for 8% -> 16%
where the time goes in v2:
time: 74.5 us; the launch traced here: 74 us
  starting transfers between devices  31.8 us (43%)
  Pallas kernels  17.9 us (24%)
  blocking collectives  11.7 us (16%)
  waiting for transfers between devices  8.41 us (11%)
  local copies, waits for them, and re-layouts  2.37 us (3%)
  other arithmetic  0.97 us (1%)
  between operations  0.8 us (1%)
    ppermute x6, starting transfers between devices, shards(): move = lambda x, route: lax.ppermute(x, 'task', route)  31.8 us
    all_to_all x1, blocking collectives, shards(): arrived = lax.all_to_all(sent, 'aux', 0, 0, tiled=True)  11.7 us
    pallas_call x1, Pallas kernels, early_tiles(): pl.pallas_call(early_kernel, out_shape=(jax.ShapeDtypeStruct((slots, PAIR...  8.95 us
    ppermute x6, waiting for transfers between devices, shards(): move = lambda x, route: lax.ppermute(x, 'task', route)  8.41 us
    pallas_call x1, Pallas kernels, all_terms(): pl.pallas_call(late_kernel, out_shape=(jax.ShapeDtypeStruct((parts, occup...  6.27 us
    unnamed x8, local copies, waits for them, and re-layouts  2.28 us
    pallas_call x1, Pallas kernels, pack(): pl.pallas_call(pack_kernel, out_shape=(jax.ShapeDtypeStruct((fac.shape[0]...  2.09 us
  transfers between devices with their start and end apart: 6, of which 3 were waited for; matrix products, arithmetic and copies ran while one was open for 0% of the time, Pallas kernels for 16%

profile of v2, /device:TPU:2, one launch (start us, length us, event | category | flops | bytes accessed | tf_op | source)
XLA Modules:
  0.0 74.0 jit_solution(1220768300083682454)
XLA Ops:
  0.0 0.0 copy-start.3
  0.0 14.0 %collective-permute-start.1 = (bf16[512,1024]{1,0:T(8,128)(2,1)}, bf16[512,1024]{1,0:T(8,128)(2,1)}, u32[]{:S(2)}, u32[]{:S(2)}) collective-permute-start(bf16[512,1024]{1,0:T(8,128)(2,1)} %bitcast.8), channel_id=1, source_target_pairs={{8,0},{508,4},{16,8},{4,12},{24,16},{12,20},{32,24},{20,28},{40,32... | collective-permute-start | bytes 3145736 | tf_op jit(solution)/shard_map/ppermute | solution.py:329
  14.0 0.0 copy-start.1
  14.0 1.2 %copy-done.1 = bf16[1,512,1024]{2,1,0:T(8,128)(2,1)S(1)} copy-done((bf16[1,512,1024]{2,1,0:T(8,128)(2,1)S(1)}, bf16[1,512,1024]{2,1,0:T(8,128)(2,1)}, u32[]{:S(2)}) %copy-start.1) | copy-done | bytes 1048600
  15.2 0.0 copy-start.2
  15.2 1.0 %copy-done.2 = bf16[1,256,1024]{2,1,0:T(8,128)(2,1)S(1)} copy-done((bf16[1,256,1024]{2,1,0:T(8,128)(2,1)S(1)}, bf16[1,256,1024]{2,1,0:T(8,128)(2,1)}, u32[]{:S(2)}) %copy-start.2) | copy-done | bytes 524312
  16.3 2.1 %pack.1 = (bf16[768,1024]{1,0:T(8,128)(2,1)S(1)}, bf16[256,1024]{1,0:T(8,128)(2,1)}) custom-call(bf16[512,1024]{1,0:T(8,128)(2,1)S(1)} %bitcast.9, bf16[256,1024]{1,0:T(8,128)(2,1)S(1)} %bitcast.10), custom_call_target="tpu_custom_call" | custom-call | flops 1 | bytes 1 | tf_op jit(solution)/shard_map/pack/pallas_call | solution.py:56
  18.4 1.9 %collective-permute-start = (bf16[768,1024]{1,0:T(8,128)(2,1)S(1)}, bf16[768,1024]{1,0:T(8,128)(2,1)S(1)}, u32[]{:S(2)}, u32[]{:S(2)}) collective-permute-start(bf16[768,1024]{1,0:T(8,128)(2,1)S(1)} %get-tuple-element.12.own), channel_id=1, source_target_pairs={{4,0},{0,4},{12,8},{8,12},{20,16},{16,20},{28,24},{24,28},{36,32},... | collective-permute-start | bytes 4718600 | tf_op jit(solution)/shard_map/ppermute | solution.py:329
  20.3 1.9 %collective-permute-start.3 = (bf16[768,1024]{1,0:T(8,128)(2,1)S(1)}, bf16[768,1024]{1,0:T(8,128)(2,1)}, u32[]{:S(2)}, u32[]{:S(2)}) collective-permute-start(bf16[768,1024]{1,0:T(8,128)(2,1)S(1)} %get-tuple-element.12.own), channel_id=1, source_target_pairs={{504,0},{12,4},{0,8},{20,12},{8,16},{28,20},{16,24},{36,28},{24,32... | collective-permute-start | bytes 4718600 | tf_op jit(solution)/shard_map/ppermute | solution.py:329
  22.2 6.7 %collective-permute-done.1.near = bf16[512,1024]{1,0:T(8,128)(2,1)} collective-permute-done((bf16[512,1024]{1,0:T(8,128)(2,1)}, bf16[512,1024]{1,0:T(8,128)(2,1)}, u32[]{:S(2)}, u32[]{:S(2)}) %collective-permute-start.1) | collective-permute-done | bytes 1048608 | tf_op jit(solution)/shard_map/ppermute | solution.py:329
  28.9 1.9 %collective-permute-start.2 = (bf16[512,1024]{1,0:T(8,128)(2,1)}, bf16[512,1024]{1,0:T(8,128)(2,1)}, u32[]{:S(2)}, u32[]{:S(2)}) collective-permute-start(bf16[512,1024]{1,0:T(8,128)(2,1)} %collective-permute-done.1.near), channel_id=1, source_target_pairs={{4,0},{0,4},{12,8},{8,12},{20,16},{16,20},{28,24},{24,28},{36,32},... | collective-permute-start | bytes 3145736 | tf_op jit(solution)/shard_map/ppermute | solution.py:329
  30.8 7.7 %collective-permute-start.4 = (bf16[256,1024]{1,0:T(8,128)(2,1)}, bf16[256,1024]{1,0:T(8,128)(2,1)}, u32[]{:S(2)}, u32[]{:S(2)}) collective-permute-start(bf16[256,1024]{1,0:T(8,128)(2,1)} %get-tuple-element.15), channel_id=1, source_target_pairs={{8,0},{508,4},{16,8},{4,12},{24,16},{12,20},{32,24},{20,28},{40,32... | collective-permute-start | bytes 1572872 | tf_op jit(solution)/shard_map/ppermute | solution.py:329
  39.2 0.0 copy-done.3
  39.2 0.1 copy.5
  39.3 0.1 select_select_fusion
  39.4 0.1 pad_add_fusion.table
  39.4 0.0 collective-permute-done.partner
  39.4 0.0 collective-permute-done.2.partner_near
  39.5 9.0 %early.1 = (bf16[4,1024,1024]{2,1,0:T(8,128)(2,1)S(1)}, bf16[4,1024,512]{2,1,0:T(8,128)(2,1)S(1)}) custom-call(s32[4,4]{1,0:T(4,128)S(1)} %pad_add_fusion.table, bf16[768,1024]{1,0:T(8,128)(2,1)S(1)} %get-tuple-element.12.own, bf16[768,1024]{1,0:T(8,128)(2,1)S(1)} %collective-permute-done.partner, bf16[512,1024]{1,0:T(8,128)(2,1)} %collective-permute-done.1.near, ...), custom_call_target="tpu_custom_call" | custom-call | flops 1 | bytes 1 | tf_op jit(solution)/shard_map/early/pallas_call | solution.py:255
  48.4 0.0 copy-start
  48.4 0.6 collective-permute-done.4.amp_2
  49.1 4.4 %collective-permute-start.5 = (bf16[256,1024]{1,0:T(8,128)(2,1)}, bf16[256,1024]{1,0:T(8,128)(2,1)S(1)}, u32[]{:S(2)}, u32[]{:S(2)}) collective-permute-start(bf16[256,1024]{1,0:T(8,128)(2,1)} %collective-permute-done.4.amp_2), channel_id=1, source_target_pairs={{4,0},{0,4},{12,8},{8,12},{20,16},{16,20},{28,24},{24,28},{36,32},... | collective-permute-start | bytes 1572872 | tf_op jit(solution)/shard_map/ppermute | solution.py:329
  53.5 0.0 collective-permute-done.3.far
  53.5 0.6 turn.1.far_turned
  54.1 0.0 copy-done
  54.1 1.1 %collective-permute-done.5.amp_4 = bf16[256,1024]{1,0:T(8,128)(2,1)S(1)} collective-permute-done((bf16[256,1024]{1,0:T(8,128)(2,1)}, bf16[256,1024]{1,0:T(8,128)(2,1)S(1)}, u32[]{:S(2)}, u32[]{:S(2)}) %collective-permute-start.5) | collective-permute-done | bytes 524320 | tf_op jit(solution)/shard_map/ppermute | solution.py:329
  55.2 6.3 %late.1 = (bf16[4,256,256]{2,1,0:T(8,128)(2,1)S(1)}, f32[256,256]{1,0:T(8,128)S(1)}) custom-call(s32[4,4]{1,0:T(4,128)S(1)} %pad_add_fusion.table, bf16[4,1024,1024]{2,1,0:T(8,128)(2,1)} %copy-done, bf16[4,1024,512]{2,1,0:T(8,128)(2,1)S(1)} %get-tuple-element.14.early_turned, bf16[1024,512]{1,0:T(8,128)(2,1)S(1)} %turn.1.far_turned, ...), custom_call_target="tpu_custom_call" | custom-call | flops 1 | bytes 1 | tf_op jit(solution)/shard_map/late/pallas_call | solution.py:297
  61.5 11.7 %all_to_all.5 = bf16[4,256,256]{2,1,0:T(8,128)(2,1)S(1)} all-to-all(bf16[4,256,256]{2,1,0:T(8,128)(2,1)S(1)} %get-tuple-element.18), channel_id=1, replica_groups=mesh['task'=128,'aux'=4] {'aux'}, dimensions={0} | all-to-all | bytes 1048576 | tf_op jit(solution)/shard_map/all_to_all | solution.py:356
  73.2 0.1 convert_reduce_fusion
  73.2 0.7 add_bitcast_fusion
  (2 shorter events, 0.0 us)
Async XLA Ops:
  0.0 39.2 %copy-start.3 = (s32[1,4,3]{1,0,2:T(1,128)S(1)}, s32[1,4,3]{1,0,2:T(1,128)}, u32[]{:S(2)}) copy-start(s32[1,4,3]{1,0,2:T(1,128)} %param.7) | copy-start | bytes 148
  0.0 28.9 %collective-permute-start.1 = (bf16[512,1024]{1,0:T(8,128)(2,1)}, bf16[512,1024]{1,0:T(8,128)(2,1)}, u32[]{:S(2)}, u32[]{:S(2)}) collective-permute-start(bf16[512,1024]{1,0:T(8,128)(2,1)} %bitcast.8), channel_id=1, source_target_pairs={{8,0},{508,4},{16,8},{4,12},{24,16},{12,20},{32,24},{20,28},{40,32... | collective-permute-start | bytes 3145736 | tf_op jit(solution)/shard_map/ppermute | solution.py:329
  14.0 1.2 %copy-start.1 = (bf16[1,512,1024]{2,1,0:T(8,128)(2,1)S(1)}, bf16[1,512,1024]{2,1,0:T(8,128)(2,1)}, u32[]{:S(2)}) copy-start(bf16[1,512,1024]{2,1,0:T(8,128)(2,1)} %param.4) | copy-start | bytes 3145732
  15.2 1.0 %copy-start.2 = (bf16[1,256,1024]{2,1,0:T(8,128)(2,1)S(1)}, bf16[1,256,1024]{2,1,0:T(8,128)(2,1)}, u32[]{:S(2)}) copy-start(bf16[1,256,1024]{2,1,0:T(8,128)(2,1)} %param.5) | copy-start | bytes 1572868
  18.4 21.1 %collective-permute-start = (bf16[768,1024]{1,0:T(8,128)(2,1)S(1)}, bf16[768,1024]{1,0:T(8,128)(2,1)S(1)}, u32[]{:S(2)}, u32[]{:S(2)}) collective-permute-start(bf16[768,1024]{1,0:T(8,128)(2,1)S(1)} %get-tuple-element.12.own), channel_id=1, source_target_pairs={{4,0},{0,4},{12,8},{8,12},{20,16},{16,20},{28,24},{24,28},{36,32},... | collective-permute-start | bytes 4718600 | tf_op jit(solution)/shard_map/ppermute | solution.py:329
  20.3 33.2 %collective-permute-start.3 = (bf16[768,1024]{1,0:T(8,128)(2,1)S(1)}, bf16[768,1024]{1,0:T(8,128)(2,1)}, u32[]{:S(2)}, u32[]{:S(2)}) collective-permute-start(bf16[768,1024]{1,0:T(8,128)(2,1)S(1)} %get-tuple-element.12.own), channel_id=1, source_target_pairs={{504,0},{12,4},{0,8},{20,12},{8,16},{28,20},{16,24},{36,28},{24,32... | collective-permute-start | bytes 4718600 | tf_op jit(solution)/shard_map/ppermute | solution.py:329
  28.9 10.6 %collective-permute-start.2 = (bf16[512,1024]{1,0:T(8,128)(2,1)}, bf16[512,1024]{1,0:T(8,128)(2,1)}, u32[]{:S(2)}, u32[]{:S(2)}) collective-permute-start(bf16[512,1024]{1,0:T(8,128)(2,1)} %collective-permute-done.1.near), channel_id=1, source_target_pairs={{4,0},{0,4},{12,8},{8,12},{20,16},{16,20},{28,24},{24,28},{36,32},... | collective-permute-start | bytes 3145736 | tf_op jit(solution)/shard_map/ppermute | solution.py:329
  30.8 18.3 %collective-permute-start.4 = (bf16[256,1024]{1,0:T(8,128)(2,1)}, bf16[256,1024]{1,0:T(8,128)(2,1)}, u32[]{:S(2)}, u32[]{:S(2)}) collective-permute-start(bf16[256,1024]{1,0:T(8,128)(2,1)} %get-tuple-element.15), channel_id=1, source_target_pairs={{8,0},{508,4},{16,8},{4,12},{24,16},{12,20},{32,24},{20,28},{40,32... | collective-permute-start | bytes 1572872 | tf_op jit(solution)/shard_map/ppermute | solution.py:329
  48.4 5.7 %copy-start = (bf16[4,1024,1024]{2,1,0:T(8,128)(2,1)}, bf16[4,1024,1024]{2,1,0:T(8,128)(2,1)S(1)}, u32[]{:S(2)}) copy-start(bf16[4,1024,1024]{2,1,0:T(8,128)(2,1)S(1)} %get-tuple-element.13.early) | copy-start | bytes 25165828
  49.1 6.1 %collective-permute-start.5 = (bf16[256,1024]{1,0:T(8,128)(2,1)}, bf16[256,1024]{1,0:T(8,128)(2,1)S(1)}, u32[]{:S(2)}, u32[]{:S(2)}) collective-permute-start(bf16[256,1024]{1,0:T(8,128)(2,1)} %collective-permute-done.4.amp_2), channel_id=1, source_target_pairs={{4,0},{0,4},{12,8},{8,12},{20,16},{16,20},{28,24},{24,28},{36,32},... | collective-permute-start | bytes 1572872 | tf_op jit(solution)/shard_map/ppermute | solution.py:329

commit v3 on v2

--- a/solution.py
+++ b/solution.py
@@ -35,6 +35,24 @@
 
 def cost(flops, moved):
     return pl.CostEstimate(flops=flops, bytes_accessed=moved, transcendentals=0)
+
+
+def amp_kernel(amp, out, swap):
+    swap[...] = swap_matrix()
+    out[...] = jnp.dot(amp[...], swap[...], preferred_element_type=F32).astype(BF16)
+
+
+def swapped_pairs(amp):
+    return pl.pallas_call(
+        amp_kernel,
+        out_shape=jax.ShapeDtypeStruct(amp.shape, BF16),
+        in_specs=[VMEM],
+        out_specs=VMEM,
+        scratch_shapes=[pltpu.VMEM((PAIRS, PAIRS), BF16)],
+        compiler_params=params(16),
+        cost_estimate=cost(1, 1),
+        name="amp",
+    )(amp)
 
 
 def pack_kernel(fac, amp, out, amp_out, swap, fac_buf, sems):
@@ -331,14 +349,14 @@
     fac = factors[0]
     table = slot_table(task_counts, task_tiles[0])
     fac_2 = move(fac, near)
-    own, amp = pack(fac, amplitudes[0])
+    own, _ = pack(fac, amplitudes[0])
     packed_3 = move(own, far)
     packed_1 = move(own, swap)
-    amp_2 = move(amp, near)
-    fac_4 = move(fac_2, swap)
-    early, early_turned = early_tiles(table, own, packed_1, fac_2, fac_4)
-    amp_4 = move(after(amp_2, early), swap)
-    far_turned = turn_far(table, packed_3, fac.shape[0])
+    amp_2 = swapped_pairs(move(amplitudes[0], near))
+    fac_4 = move(after(fac_2, amp_2), swap)
+    amp_4 = move(amp_2, swap)
+    early, early_turned = early_tiles(after(table, amp_4), own, packed_1, fac_2, fac_4)
+    far_turned = turn_far(after(table, early), packed_3, fac.shape[0])
     sent, kept = all_terms(
         table,
         early,

time: 74.5 us -> 74.4 us (level)
  starting transfers between devices: 31.8 us -> 26 us
  waiting for transfers between devices: 8.41 us -> 12.3 us
  Pallas kernels: 17.9 us -> 19.4 us
  local copies, waits for them, and re-layouts: 2.37 us -> 3.16 us
    ppermute x6, starting transfers between devices: 31.8 us -> 26 us  [shards(): move = lambda x, route: lax.ppermute(x, 'task', route)]
    ppermute x6, waiting for transfers between devices: 8.41 us -> 12.3 us  [shards(): move = lambda x, route: lax.ppermute(x, 'task', route)]
    pallas_call x1, Pallas kernels: 0.6 us -> 3.97 us  [turn_far(): pl.pallas_call(turn_kernel, out_shape=jax.ShapeDtypeStruct((PAIRS, quarte...]
    pallas_call x1, Pallas kernels: 8.95 us -> 7.46 us  [early_tiles(): pl.pallas_call(early_kernel, out_shape=(jax.ShapeDtypeStruct((slots, PAIR...]
    pallas_call x1, Pallas kernels: 6.27 us -> 5.16 us  [all_terms(): pl.pallas_call(late_kernel, out_shape=(jax.ShapeDtypeStruct((parts, occup...]
    unnamed x8 -> x12, local copies, waits for them, and re-layouts: 2.28 us -> 3.07 us
  transfers between devices with their start and end apart: 6 -> 6, of which waited for: 3 -> 2; matrix products, arithmetic and copies ran while one was open for 0% -> 0% of each run, Pallas kernels for 16% -> 14%
where the time goes in v3:
time: 74.4 us; the launch traced here: 73.9 us
  starting transfers between devices  26 us (35%)
  Pallas kernels  19.4 us (26%)
  waiting for transfers between devices  12.3 us (17%)
  blocking collectives  11.2 us (15%)
  local copies, waits for them, and re-layouts  3.16 us (4%)
  other arithmetic  0.97 us (1%)
  between operations  0.83 us (1%)
    ppermute x6, starting transfers between devices, shards(): move = lambda x, route: lax.ppermute(x, 'task', route)  26 us
    ppermute x6, waiting for transfers between devices, shards(): move = lambda x, route: lax.ppermute(x, 'task', route)  12.3 us
    all_to_all x1, blocking collectives, shards(): arrived = lax.all_to_all(sent, 'aux', 0, 0, tiled=True)  11.2 us
    pallas_call x1, Pallas kernels, early_tiles(): pl.pallas_call(early_kernel, out_shape=(jax.ShapeDtypeStruct((slots, PAIR...  7.46 us
    pallas_call x1, Pallas kernels, all_terms(): pl.pallas_call(late_kernel, out_shape=(jax.ShapeDtypeStruct((parts, occup...  5.16 us
    pallas_call x1, Pallas kernels, turn_far(): pl.pallas_call(turn_kernel, out_shape=jax.ShapeDtypeStruct((PAIRS, quarte...  3.97 us
    unnamed x12, local copies, waits for them, and re-layouts  3.07 us
    pallas_call x1, Pallas kernels, pack(): pl.pallas_call(pack_kernel, out_shape=(jax.ShapeDtypeStruct((fac.shape[0]...  2.08 us
  transfers between devices with their start and end apart: 6, of which 2 were waited for; matrix products, arithmetic and copies ran while one was open for 0% of the time, Pallas kernels for 14%

profile of v3, /device:TPU:2, one launch (start us, length us, event | category | flops | bytes accessed | tf_op | source)
XLA Modules:
  0.0 73.9 jit_solution(9681822945591612344)
XLA Ops:
  0.0 14.0 %collective-permute-start.3 = (bf16[512,1024]{1,0:T(8,128)(2,1)}, bf16[512,1024]{1,0:T(8,128)(2,1)}, u32[]{:S(2)}, u32[]{:S(2)}) collective-permute-start(bf16[512,1024]{1,0:T(8,128)(2,1)} %bitcast.8), channel_id=1, source_target_pairs={{8,0},{508,4},{16,8},{4,12},{24,16},{12,20},{32,24},{20,28},{40,32... | collective-permute-start | bytes 3145736 | tf_op jit(solution)/shard_map/ppermute | solution.py:347
  14.0 3.3 %collective-permute-start = (bf16[256,1024]{1,0:T(8,128)(2,1)}, bf16[256,1024]{1,0:T(8,128)(2,1)S(1)}, u32[]{:S(2)}, u32[]{:S(2)}) collective-permute-start(bf16[256,1024]{1,0:T(8,128)(2,1)} %bitcast.10), channel_id=1, source_target_pairs={{8,0},{508,4},{16,8},{4,12},{24,16},{12,20},{32,24},{20,28},{40,32... | collective-permute-start | bytes 1572872 | tf_op jit(solution)/shard_map/ppermute | solution.py:347
  17.2 0.0 copy-start.3
  17.3 1.2 %copy-done.3 = bf16[1,512,1024]{2,1,0:T(8,128)(2,1)S(1)} copy-done((bf16[1,512,1024]{2,1,0:T(8,128)(2,1)S(1)}, bf16[1,512,1024]{2,1,0:T(8,128)(2,1)}, u32[]{:S(2)}) %copy-start.3) | copy-done | bytes 1048600
  18.5 1.0 %copy-done.4 = bf16[1,256,1024]{2,1,0:T(8,128)(2,1)S(1)} copy-done((bf16[1,256,1024]{2,1,0:T(8,128)(2,1)S(1)}, bf16[1,256,1024]{2,1,0:T(8,128)(2,1)}, u32[]{:S(2)}) %copy-start.4) | copy-done | bytes 524312
  19.5 2.1 %pack.1 = (bf16[768,1024]{1,0:T(8,128)(2,1)S(1)}, bf16[256,1024]{1,0:T(8,128)(2,1)}) custom-call(bf16[512,1024]{1,0:T(8,128)(2,1)S(1)} %bitcast.9, bf16[256,1024]{1,0:T(8,128)(2,1)S(1)} %bitcast.11), custom_call_target="tpu_custom_call" | custom-call | flops 1 | bytes 1 | tf_op jit(solution)/shard_map/pack/pallas_call | solution.py:74
  21.6 1.9 %collective-permute-start.2 = (bf16[768,1024]{1,0:T(8,128)(2,1)S(1)}, bf16[768,1024]{1,0:T(8,128)(2,1)S(1)}, u32[]{:S(2)}, u32[]{:S(2)}) collective-permute-start(bf16[768,1024]{1,0:T(8,128)(2,1)S(1)} %get-tuple-element.14.own), channel_id=1, source_target_pairs={{4,0},{0,4},{12,8},{8,12},{20,16},{16,20},{28,24},{24,28},{36,32},... | collective-permute-start | bytes 4718600 | tf_op jit(solution)/shard_map/ppermute | solution.py:347
  23.5 2.6 %collective-permute-start.5 = (bf16[768,1024]{1,0:T(8,128)(2,1)S(1)}, bf16[768,1024]{1,0:T(8,128)(2,1)}, u32[]{:S(2)}, u32[]{:S(2)}) collective-permute-start(bf16[768,1024]{1,0:T(8,128)(2,1)S(1)} %get-tuple-element.14.own), channel_id=1, source_target_pairs={{504,0},{12,4},{0,8},{20,12},{8,16},{28,20},{16,24},{36,28},{24,32... | collective-permute-start | bytes 4718600 | tf_op jit(solution)/shard_map/ppermute | solution.py:347
  26.1 10.7 %collective-permute-done.amp = bf16[256,1024]{1,0:T(8,128)(2,1)S(1)} collective-permute-done((bf16[256,1024]{1,0:T(8,128)(2,1)}, bf16[256,1024]{1,0:T(8,128)(2,1)S(1)}, u32[]{:S(2)}, u32[]{:S(2)}) %collective-permute-start) | collective-permute-done | bytes 524320 | tf_op jit(solution)/shard_map/ppermute | solution.py:347
  36.9 0.7 amp.1.amp_2
  37.6 0.0 copy-start.1
  37.6 0.8 %copy-done.1 = bf16[256,1024]{1,0:T(8,128)(2,1)} copy-done((bf16[256,1024]{1,0:T(8,128)(2,1)}, bf16[256,1024]{1,0:T(8,128)(2,1)S(1)}, u32[]{:S(2)}) %copy-start.1) | copy-done | bytes 524312
  38.4 0.0 collective-permute-done.3.near
  38.4 1.9 %collective-permute-start.4 = (bf16[512,1024]{1,0:T(8,128)(2,1)}, bf16[512,1024]{1,0:T(8,128)(2,1)}, u32[]{:S(2)}, u32[]{:S(2)}) collective-permute-start(bf16[512,1024]{1,0:T(8,128)(2,1)} %collective-permute-done.3.near), channel_id=1, source_target_pairs={{4,0},{0,4},{12,8},{8,12},{20,16},{16,20},{28,24},{24,28},{36,32},... | collective-permute-start | bytes 3145736 | tf_op jit(solution)/shard_map/ppermute | solution.py:347
  41.0 0.0 copy-done.5
  41.0 0.1 copy.5
  41.1 2.4 %collective-permute-start.1 = (bf16[256,1024]{1,0:T(8,128)(2,1)}, bf16[256,1024]{1,0:T(8,128)(2,1)S(1)}, u32[]{:S(2)}, u32[]{:S(2)}) collective-permute-start(bf16[256,1024]{1,0:T(8,128)(2,1)} %copy-done.1), channel_id=1, source_target_pairs={{4,0},{0,4},{12,8},{8,12},{20,16},{16,20},{28,24},{24,28},{36,32},... | collective-permute-start | bytes 1572872 | tf_op jit(solution)/shard_map/ppermute | solution.py:347
  43.5 0.1 select_select_fusion
  43.6 0.1 pad_add_fusion.table
  43.7 1.6 %collective-permute-done.1.amp_4 = bf16[256,1024]{1,0:T(8,128)(2,1)S(1)} collective-permute-done((bf16[256,1024]{1,0:T(8,128)(2,1)}, bf16[256,1024]{1,0:T(8,128)(2,1)S(1)}, u32[]{:S(2)}, u32[]{:S(2)}) %collective-permute-start.1) | collective-permute-done | bytes 524320 | tf_op jit(solution)/shard_map/ppermute | solution.py:347
  45.2 0.0 collective-permute-done.2.partner
  45.2 0.0 collective-permute-done.4.partner_near
  45.2 7.5 %early.1 = (bf16[4,1024,1024]{2,1,0:T(8,128)(2,1)S(1)}, bf16[4,1024,512]{2,1,0:T(8,128)(2,1)S(1)}) custom-call(s32[4,4]{1,0:T(4,128)S(1)} %pad_add_fusion.table, bf16[768,1024]{1,0:T(8,128)(2,1)S(1)} %get-tuple-element.14.own, bf16[768,1024]{1,0:T(8,128)(2,1)S(1)} %collective-permute-done.2.partner, bf16[512,1024]{1,0:T(8,128)(2,1)} %collective-permute-done.3.near, ...), custom_call_target="tpu_custom_call" | custom-call | flops 1 | bytes 1 | tf_op jit(solution)/shard_map/early/pallas_call | solution.py:273
  52.7 0.0 copy-start
  52.7 0.0 copy-start.2
  52.7 0.0 collective-permute-done.5.far
  52.7 4.0 %turn.1.far_turned = bf16[1024,512]{1,0:T(8,128)(2,1)S(1)} custom-call(s32[4,4]{1,0:T(4,128)S(1)} %pad_add_fusion.table, bf16[768,1024]{1,0:T(8,128)(2,1)} %collective-permute-done.5.far), custom_call_target="tpu_custom_call" | custom-call | flops 10737418240 | bytes 1048576 | tf_op jit(solution)/shard_map/turn/pallas_call | solution.py:296
  56.7 0.0 copy-done
  56.7 5.2 %late.1 = (bf16[4,256,256]{2,1,0:T(8,128)(2,1)S(1)}, f32[256,256]{1,0:T(8,128)S(1)}) custom-call(s32[4,4]{1,0:T(4,128)S(1)} %pad_add_fusion.table, bf16[4,1024,1024]{2,1,0:T(8,128)(2,1)} %copy-done, bf16[4,1024,512]{2,1,0:T(8,128)(2,1)S(1)} %get-tuple-element.17.early_turned, bf16[1024,512]{1,0:T(8,128)(2,1)S(1)} %turn.1.far_turned, ...), custom_call_target="tpu_custom_call" | custom-call | flops 1 | bytes 1 | tf_op jit(solution)/shard_map/late/pallas_call | solution.py:315
  61.9 11.2 %all_to_all.5 = bf16[4,256,256]{2,1,0:T(8,128)(2,1)S(1)} all-to-all(bf16[4,256,256]{2,1,0:T(8,128)(2,1)S(1)} %get-tuple-element.20), channel_id=1, replica_groups=mesh['task'=128,'aux'=4] {'aux'}, dimensions={0} | all-to-all | bytes 1048576 | tf_op jit(solution)/shard_map/all_to_all | solution.py:374
  73.1 0.1 convert_reduce_fusion
  73.2 0.7 add_bitcast_fusion
  (5 shorter events, 0.0 us)
Async XLA Ops:
  0.0 41.0 %copy-start.5 = (s32[1,4,3]{1,0,2:T(1,128)S(1)}, s32[1,4,3]{1,0,2:T(1,128)}, u32[]{:S(2)}) copy-start(s32[1,4,3]{1,0,2:T(1,128)} %param.7) | copy-start | bytes 148
  0.0 38.4 %collective-permute-start.3 = (bf16[512,1024]{1,0:T(8,128)(2,1)}, bf16[512,1024]{1,0:T(8,128)(2,1)}, u32[]{:S(2)}, u32[]{:S(2)}) collective-permute-start(bf16[512,1024]{1,0:T(8,128)(2,1)} %bitcast.8), channel_id=1, source_target_pairs={{8,0},{508,4},{16,8},{4,12},{24,16},{12,20},{32,24},{20,28},{40,32... | collective-permute-start | bytes 3145736 | tf_op jit(solution)/shard_map/ppermute | solution.py:347
  14.0 22.9 %collective-permute-start = (bf16[256,1024]{1,0:T(8,128)(2,1)}, bf16[256,1024]{1,0:T(8,128)(2,1)S(1)}, u32[]{:S(2)}, u32[]{:S(2)}) collective-permute-start(bf16[256,1024]{1,0:T(8,128)(2,1)} %bitcast.10), channel_id=1, source_target_pairs={{8,0},{508,4},{16,8},{4,12},{24,16},{12,20},{32,24},{20,28},{40,32... | collective-permute-start | bytes 1572872 | tf_op jit(solution)/shard_map/ppermute | solution.py:347
  17.2 1.2 %copy-start.3 = (bf16[1,512,1024]{2,1,0:T(8,128)(2,1)S(1)}, bf16[1,512,1024]{2,1,0:T(8,128)(2,1)}, u32[]{:S(2)}) copy-start(bf16[1,512,1024]{2,1,0:T(8,128)(2,1)} %param.4) | copy-start | bytes 3145732
  18.5 1.0 %copy-start.4 = (bf16[1,256,1024]{2,1,0:T(8,128)(2,1)S(1)}, bf16[1,256,1024]{2,1,0:T(8,128)(2,1)}, u32[]{:S(2)}) copy-start(bf16[1,256,1024]{2,1,0:T(8,128)(2,1)} %param.5) | copy-start | bytes 1572868
  21.6 23.6 %collective-permute-start.2 = (bf16[768,1024]{1,0:T(8,128)(2,1)S(1)}, bf16[768,1024]{1,0:T(8,128)(2,1)S(1)}, u32[]{:S(2)}, u32[]{:S(2)}) collective-permute-start(bf16[768,1024]{1,0:T(8,128)(2,1)S(1)} %get-tuple-element.14.own), channel_id=1, source_target_pairs={{4,0},{0,4},{12,8},{8,12},{20,16},{16,20},{28,24},{24,28},{36,32},... | collective-permute-start | bytes 4718600 | tf_op jit(solution)/shard_map/ppermute | solution.py:347
  23.5 29.2 %collective-permute-start.5 = (bf16[768,1024]{1,0:T(8,128)(2,1)S(1)}, bf16[768,1024]{1,0:T(8,128)(2,1)}, u32[]{:S(2)}, u32[]{:S(2)}) collective-permute-start(bf16[768,1024]{1,0:T(8,128)(2,1)S(1)} %get-tuple-element.14.own), channel_id=1, source_target_pairs={{504,0},{12,4},{0,8},{20,12},{8,16},{28,20},{16,24},{36,28},{24,32... | collective-permute-start | bytes 4718600 | tf_op jit(solution)/shard_map/ppermute | solution.py:347
  37.6 0.8 %copy-start.1 = (bf16[256,1024]{1,0:T(8,128)(2,1)}, bf16[256,1024]{1,0:T(8,128)(2,1)S(1)}, u32[]{:S(2)}) copy-start(bf16[256,1024]{1,0:T(8,128)(2,1)S(1)} %amp.1.amp_2) | copy-start | bytes 1572868
  38.4 6.8 %collective-permute-start.4 = (bf16[512,1024]{1,0:T(8,128)(2,1)}, bf16[512,1024]{1,0:T(8,128)(2,1)}, u32[]{:S(2)}, u32[]{:S(2)}) collective-permute-start(bf16[512,1024]{1,0:T(8,128)(2,1)} %collective-permute-done.3.near), channel_id=1, source_target_pairs={{4,0},{0,4},{12,8},{8,12},{20,16},{16,20},{28,24},{24,28},{36,32},... | collective-permute-start | bytes 3145736 | tf_op jit(solution)/shard_map/ppermute | solution.py:347
  41.1 4.1 %collective-permute-start.1 = (bf16[256,1024]{1,0:T(8,128)(2,1)}, bf16[256,1024]{1,0:T(8,128)(2,1)S(1)}, u32[]{:S(2)}, u32[]{:S(2)}) collective-permute-start(bf16[256,1024]{1,0:T(8,128)(2,1)} %copy-done.1), channel_id=1, source_target_pairs={{4,0},{0,4},{12,8},{8,12},{20,16},{16,20},{28,24},{24,28},{36,32},... | collective-permute-start | bytes 1572872 | tf_op jit(solution)/shard_map/ppermute | solution.py:347
  52.7 4.0 %copy-start = (bf16[4,1024,1024]{2,1,0:T(8,128)(2,1)}, bf16[4,1024,1024]{2,1,0:T(8,128)(2,1)S(1)}, u32[]{:S(2)}) copy-start(bf16[4,1024,1024]{2,1,0:T(8,128)(2,1)S(1)} %get-tuple-element.16.early) | copy-start | bytes 25165828
  52.7 4.0 %copy-start.2 = (bf16[256,1024]{1,0:T(8,128)(2,1)S(1)}, bf16[256,1024]{1,0:T(8,128)(2,1)}, u32[]{:S(2)}) copy-start(bf16[256,1024]{1,0:T(8,128)(2,1)} %copy-done.1) | copy-start | bytes 1572868

commit v4 on v3

--- a/solution.py
+++ b/solution.py
@@ -189,45 +189,25 @@
         pl.when(half(slot))(lambda: turned_copy(slot).wait())
 
 
-def turn_kernel(table, far, out, swap, fac, turned, sems):
-    slots = table.shape[0]
-
-    @pl.when(any_slot(lambda s: table[s, 0] == SECOND, slots))
-    def _():
-        arrive = pltpu.make_async_copy(far.at[: fac.shape[0]], fac, sems.at[0])
-        arrive.start()
-        swap[...] = swap_matrix()
-        arrive.wait()
-        turned[...] = turn(swap, fac[...])
-        leave = pltpu.make_async_copy(turned, out, sems.at[1])
-        leave.start()
-        leave.wait()
-
-
 def late_kernel(
-    table, early, early_turned, far_turned, own, partner, near, partner_near, far, amp_2, amp_4, *refs
+    table, early, early_turned, own, partner, near, partner_near, far, amp_2, amp_4, *refs
 ):
-    sent, kept, total, amp_buf, left, turned, tiles, sems = refs
+    sent, kept, total, amp_buf, left, right, turned, swap, tiles, sems, far_sem = refs
     depth, slots = near.shape[0], table.shape[0]
     facs = {0: own.at[:depth], 1: partner.at[:depth], 2: near, 3: far.at[:depth], 4: partner_near}
     amps = {0: own.at[depth:], 1: partner.at[depth:], 2: amp_2, 3: far.at[depth:], 4: amp_4}
     live = lambda s: table[s, 0] != EMPTY
     mine = lambda s: table[s, 0] >= FIRST
     made = lambda s: table[s, 0] == READY
+    some = any_slot(lambda s: table[s, 0] == SECOND, slots)
+    far_copy = pltpu.make_async_copy(facs[FAR], right, far_sem.at[0])
+    turned_copy = lambda s: pltpu.make_async_copy(early_turned.at[s], turned.at[s], sems.at[s, 1])
+    pl.when(some)(lambda: far_copy.start())
     for slot in range(slots):
+        pl.when(table[slot, 0] == FIRST)(lambda: turned_copy(slot).start())
 
         @pl.when(mine(slot))
         def _():
-            right_far = table[slot, 0] == SECOND
-
-            @pl.when(right_far)
-            def _():
-                pltpu.make_async_copy(far_turned, turned.at[slot], sems.at[slot, 1]).start()
-
-            @pl.when(jnp.logical_not(right_far))
-            def _():
-                pltpu.make_async_copy(early_turned.at[slot], turned.at[slot], sems.at[slot, 1]).start()
-
             start_one(table[slot, 1], facs, left.at[slot], sems.at[slot, 0])
 
         @pl.when(made(slot))
@@ -239,14 +219,22 @@
             start_one(table[slot, 3], amps, amp_buf.at[slot], sems.at[slot, 3])
 
     total[...] = jnp.zeros_like(total)
+
+    @pl.when(some)
+    def _():
+        swap[...] = swap_matrix()
+        far_copy.wait()
+        turned[slots] = turn(swap, right[...])
 
     @pl.loop(0, slots)
     def _(slot):
+        pl.when(table[slot, 0] == FIRST)(lambda: turned_copy(slot).wait())
+
         @pl.when(mine(slot))
         def _():
-            pltpu.make_async_copy(far_turned, turned.at[slot], sems.at[slot, 1]).wait()
             pltpu.make_async_copy(near, left.at[slot], sems.at[slot, 0]).wait()
-            product = jnp.dot(turned[slot], left[slot], preferred_element_type=F32)
+            place = jnp.where(table[slot, 0] == SECOND, slots, slot)
+            product = jnp.dot(turned[place], left[slot], preferred_element_type=F32)
             write_tile(product.astype(BF16), tiles.at[slot])
 
         @pl.when(made(slot))
@@ -292,25 +280,7 @@
     )(table, own, partner, near, partner_near)
 
 
-def turn_far(table, far, quarter):
-    return pl.pallas_call(
-        turn_kernel,
-        out_shape=jax.ShapeDtypeStruct((PAIRS, quarter), BF16),
-        in_specs=[SMEM, HBM],
-        out_specs=HBM,
-        scratch_shapes=[
-            pltpu.VMEM((PAIRS, PAIRS), BF16),
-            pltpu.VMEM((quarter, PAIRS), BF16),
-            pltpu.VMEM((PAIRS, quarter), BF16),
-            pltpu.SemaphoreType.DMA((2,)),
-        ],
-        compiler_params=params(34),
-        cost_estimate=cost(20 * quarter * PAIRS * PAIRS, 1 << 20),
-        name="turn",
-    )(table, far)
-
-
-def all_terms(table, early, early_turned, far_turned, own, partner, near, partner_near, far, amp_2, amp_4, parts):
+def all_terms(table, early, early_turned, own, partner, near, partner_near, far, amp_2, amp_4, parts):
     slots, columns, occupied, quarter = table.shape[0], PAIRS // parts, amp_2.shape[0], near.shape[0]
     return pl.pallas_call(
         late_kernel,
@@ -318,20 +288,23 @@
             jax.ShapeDtypeStruct((parts, occupied, columns), BF16),
             jax.ShapeDtypeStruct((occupied, columns), F32),
         ),
-        in_specs=[SMEM] + [HBM] * 10,
+        in_specs=[SMEM] + [HBM] * 9,
         out_specs=(VMEM, VMEM),
         scratch_shapes=[
             pltpu.VMEM((occupied, PAIRS), F32),
             pltpu.VMEM((slots, occupied, PAIRS), BF16),
             pltpu.VMEM((slots, quarter, PAIRS), BF16),
-            pltpu.VMEM((slots, PAIRS, quarter), BF16),
+            pltpu.VMEM((quarter, PAIRS), BF16),
+            pltpu.VMEM((slots + 1, PAIRS, quarter), BF16),
+            pltpu.VMEM((PAIRS, PAIRS), BF16),
             pltpu.VMEM((slots, PAIRS, PAIRS), BF16),
             pltpu.SemaphoreType.DMA((slots, 4)),
+            pltpu.SemaphoreType.DMA((1,)),
         ],
-        compiler_params=params(34),
+        compiler_params=params(29),
         cost_estimate=cost(1, 1),
         name="late",
-    )(table, early, early_turned, far_turned, own, partner, near, partner_near, far, amp_2, amp_4)
+    )(table, early, early_turned, own, partner, near, partner_near, far, amp_2, amp_4)
 
 
 def after(x, *others):
@@ -356,12 +329,10 @@
     fac_4 = move(after(fac_2, amp_2), swap)
     amp_4 = move(amp_2, swap)
     early, early_turned = early_tiles(after(table, amp_4), own, packed_1, fac_2, fac_4)
-    far_turned = turn_far(after(table, early), packed_3, fac.shape[0])
     sent, kept = all_terms(
         table,
         early,
         early_turned,
-        far_turned,
         own,
         packed_1,
         fac_2,

time: 74.4 us -> 75.1 us (level)
  the two profiles are of different devices: /device:TPU:2 before, /device:TPU:1 now
where the time goes in v4:
time: 75.1 us; the launch traced here: 76.6 us
  starting transfers between devices  33.3 us (44%)
  Pallas kernels  18.2 us (24%)
  blocking collectives  13.8 us (18%)
  waiting for transfers between devices  6.47 us (9%)
  local copies, waits for them, and re-layouts  3.15 us (4%)
  other arithmetic  0.97 us (1%)
  between operations  0.8 us (1%)
    ppermute x6, starting transfers between devices, shards(): move = lambda x, route: lax.ppermute(x, 'task', route)  33.3 us
    all_to_all x1, blocking collectives, shards(): arrived = lax.all_to_all(sent, 'aux', 0, 0, tiled=True)  13.8 us
    pallas_call x1, Pallas kernels, early_tiles(): pl.pallas_call(early_kernel, out_shape=(jax.ShapeDtypeStruct((slots, PAIR...  8.14 us
    pallas_call x1, Pallas kernels, all_terms(): pl.pallas_call(late_kernel, out_shape=(jax.ShapeDtypeStruct((parts, occup...  7.22 us
    ppermute x6, waiting for transfers between devices, shards(): move = lambda x, route: lax.ppermute(x, 'task', route)  6.47 us
    unnamed x10, local copies, waits for them, and re-layouts  3.06 us
    pallas_call x1, Pallas kernels, pack(): pl.pallas_call(pack_kernel, out_shape=(jax.ShapeDtypeStruct((fac.shape[0]...  2.07 us
  transfers between devices with their start and end apart: 6, of which 2 were waited for; matrix products, arithmetic and copies ran while one was open for 0% of the time, Pallas kernels for 14%

profile of v4, /device:TPU:1, one launch (start us, length us, event | category | flops | bytes accessed | tf_op | source)
XLA Modules:
  0.0 76.6 jit_solution(8569435067734587769)
XLA Ops:
  0.0 0.0 copy-start.4
  0.0 4.2 %collective-permute-start.3 = (bf16[512,1024]{1,0:T(8,128)(2,1)}, bf16[512,1024]{1,0:T(8,128)(2,1)}, u32[]{:S(2)}, u32[]{:S(2)}) collective-permute-start(bf16[512,1024]{1,0:T(8,128)(2,1)} %bitcast.8), channel_id=1, source_target_pairs={{8,0},{508,4},{16,8},{4,12},{24,16},{12,20},{32,24},{20,28},{40,32... | collective-permute-start | bytes 3145736 | tf_op jit(solution)/shard_map/ppermute | solution.py:320
  4.2 3.2 %collective-permute-start = (bf16[256,1024]{1,0:T(8,128)(2,1)}, bf16[256,1024]{1,0:T(8,128)(2,1)S(1)}, u32[]{:S(2)}, u32[]{:S(2)}) collective-permute-start(bf16[256,1024]{1,0:T(8,128)(2,1)} %bitcast.10), channel_id=1, source_target_pairs={{8,0},{508,4},{16,8},{4,12},{24,16},{12,20},{32,24},{20,28},{40,32... | collective-permute-start | bytes 1572872 | tf_op jit(solution)/shard_map/ppermute | solution.py:320
  7.4 0.0 copy-start.2
  7.4 1.2 %copy-done.2 = bf16[1,512,1024]{2,1,0:T(8,128)(2,1)S(1)} copy-done((bf16[1,512,1024]{2,1,0:T(8,128)(2,1)S(1)}, bf16[1,512,1024]{2,1,0:T(8,128)(2,1)}, u32[]{:S(2)}) %copy-start.2) | copy-done | bytes 1048600
  8.6 0.0 copy-start.3
  8.6 1.0 %copy-done.3 = bf16[1,256,1024]{2,1,0:T(8,128)(2,1)S(1)} copy-done((bf16[1,256,1024]{2,1,0:T(8,128)(2,1)S(1)}, bf16[1,256,1024]{2,1,0:T(8,128)(2,1)}, u32[]{:S(2)}) %copy-start.3) | copy-done | bytes 524312
  9.6 2.1 %pack.1 = (bf16[768,1024]{1,0:T(8,128)(2,1)S(1)}, bf16[256,1024]{1,0:T(8,128)(2,1)}) custom-call(bf16[512,1024]{1,0:T(8,128)(2,1)S(1)} %bitcast.9, bf16[256,1024]{1,0:T(8,128)(2,1)S(1)} %bitcast.11), custom_call_target="tpu_custom_call" | custom-call | flops 1 | bytes 1 | tf_op jit(solution)/shard_map/pack/pallas_call | solution.py:74
  11.7 13.3 %collective-permute-start.2 = (bf16[768,1024]{1,0:T(8,128)(2,1)S(1)}, bf16[768,1024]{1,0:T(8,128)(2,1)S(1)}, u32[]{:S(2)}, u32[]{:S(2)}) collective-permute-start(bf16[768,1024]{1,0:T(8,128)(2,1)S(1)} %get-tuple-element.13.own), channel_id=1, source_target_pairs={{4,0},{0,4},{12,8},{8,12},{20,16},{16,20},{28,24},{24,28},{36,32},... | collective-permute-start | bytes 4718600 | tf_op jit(solution)/shard_map/ppermute | solution.py:320
  25.0 3.0 %collective-permute-start.5 = (bf16[768,1024]{1,0:T(8,128)(2,1)S(1)}, bf16[768,1024]{1,0:T(8,128)(2,1)}, u32[]{:S(2)}, u32[]{:S(2)}) collective-permute-start(bf16[768,1024]{1,0:T(8,128)(2,1)S(1)} %get-tuple-element.13.own), channel_id=1, source_target_pairs={{504,0},{12,4},{0,8},{20,12},{8,16},{28,20},{16,24},{36,28},{24,32... | collective-permute-start | bytes 4718600 | tf_op jit(solution)/shard_map/ppermute | solution.py:320
  28.0 4.5 %collective-permute-done.amp = bf16[256,1024]{1,0:T(8,128)(2,1)S(1)} collective-permute-done((bf16[256,1024]{1,0:T(8,128)(2,1)}, bf16[256,1024]{1,0:T(8,128)(2,1)S(1)}, u32[]{:S(2)}, u32[]{:S(2)}) %collective-permute-start) | collective-permute-done | bytes 524320 | tf_op jit(solution)/shard_map/ppermute | solution.py:320
  32.5 0.7 amp.1.amp_2
  33.3 0.0 copy-start
  33.3 0.8 %copy-done = bf16[256,1024]{1,0:T(8,128)(2,1)} copy-done((bf16[256,1024]{1,0:T(8,128)(2,1)}, bf16[256,1024]{1,0:T(8,128)(2,1)S(1)}, u32[]{:S(2)}) %copy-start) | copy-done | bytes 524312
  34.1 0.0 collective-permute-done.3.near
  34.1 7.7 %collective-permute-start.4 = (bf16[512,1024]{1,0:T(8,128)(2,1)}, bf16[512,1024]{1,0:T(8,128)(2,1)}, u32[]{:S(2)}, u32[]{:S(2)}) collective-permute-start(bf16[512,1024]{1,0:T(8,128)(2,1)} %collective-permute-done.3.near), channel_id=1, source_target_pairs={{4,0},{0,4},{12,8},{8,12},{20,16},{16,20},{28,24},{24,28},{36,32},... | collective-permute-start | bytes 3145736 | tf_op jit(solution)/shard_map/ppermute | solution.py:320
  42.5 0.0 copy-done.4
  42.5 0.1 copy.5
  42.6 1.9 %collective-permute-start.1 = (bf16[256,1024]{1,0:T(8,128)(2,1)}, bf16[256,1024]{1,0:T(8,128)(2,1)S(1)}, u32[]{:S(2)}, u32[]{:S(2)}) collective-permute-start(bf16[256,1024]{1,0:T(8,128)(2,1)} %copy-done), channel_id=1, source_target_pairs={{4,0},{0,4},{12,8},{8,12},{20,16},{16,20},{28,24},{24,28},{36,32},... | collective-permute-start | bytes 1572872 | tf_op jit(solution)/shard_map/ppermute | solution.py:320
  44.5 0.1 select_select_fusion
  44.6 0.1 pad_add_fusion.table
  44.7 0.0 copy-start.1
  44.7 1.9 %collective-permute-done.1.amp_4 = bf16[256,1024]{1,0:T(8,128)(2,1)S(1)} collective-permute-done((bf16[256,1024]{1,0:T(8,128)(2,1)}, bf16[256,1024]{1,0:T(8,128)(2,1)S(1)}, u32[]{:S(2)}, u32[]{:S(2)}) %collective-permute-start.1) | collective-permute-done | bytes 524320 | tf_op jit(solution)/shard_map/ppermute | solution.py:320
  46.6 0.0 collective-permute-done.2.partner
  46.6 0.0 collective-permute-done.4.partner_near
  46.6 8.1 %early.1 = (bf16[4,1024,1024]{2,1,0:T(8,128)(2,1)S(1)}, bf16[4,1024,512]{2,1,0:T(8,128)(2,1)S(1)}) custom-call(s32[4,4]{1,0:T(4,128)S(1)} %pad_add_fusion.table, bf16[768,1024]{1,0:T(8,128)(2,1)S(1)} %get-tuple-element.13.own, bf16[768,1024]{1,0:T(8,128)(2,1)S(1)} %collective-permute-done.2.partner, bf16[512,1024]{1,0:T(8,128)(2,1)} %collective-permute-done.3.near, ...), custom_call_target="tpu_custom_call" | custom-call | flops 1 | bytes 1 | tf_op jit(solution)/shard_map/early/pallas_call | solution.py:261
  54.8 0.0 collective-permute-done.5.far
  54.8 0.0 copy-done.1
  54.8 7.2 %late.1 = (bf16[4,256,256]{2,1,0:T(8,128)(2,1)S(1)}, f32[256,256]{1,0:T(8,128)S(1)}) custom-call(s32[4,4]{1,0:T(4,128)S(1)} %pad_add_fusion.table, bf16[4,1024,1024]{2,1,0:T(8,128)(2,1)S(1)} %get-tuple-element.15.early, bf16[4,1024,512]{2,1,0:T(8,128)(2,1)S(1)} %get-tuple-element.16.early_turned, bf16[768,1024]{1,0:T(8,128)(2,1)S(1)} %get-tuple-element.13.own, ...), custom_call_target="tpu_custom_call" | custom-call | flops 1 | bytes 1 | tf_op jit(solution)/shard_map/late/pallas_call | solution.py:285
  62.0 13.8 %all_to_all.5 = bf16[4,256,256]{2,1,0:T(8,128)(2,1)S(1)} all-to-all(bf16[4,256,256]{2,1,0:T(8,128)(2,1)S(1)} %get-tuple-element.18), channel_id=1, replica_groups=mesh['task'=128,'aux'=4] {'aux'}, dimensions={0} | all-to-all | bytes 1048576 | tf_op jit(solution)/shard_map/all_to_all | solution.py:345
  75.8 0.1 convert_reduce_fusion
  75.8 0.7 add_bitcast_fusion
  (2 shorter events, 0.0 us)
Async XLA Ops:
  0.0 42.5 %copy-start.4 = (s32[1,4,3]{1,0,2:T(1,128)S(1)}, s32[1,4,3]{1,0,2:T(1,128)}, u32[]{:S(2)}) copy-start(s32[1,4,3]{1,0,2:T(1,128)} %param.7) | copy-start | bytes 148
  0.0 34.1 %collective-permute-start.3 = (bf16[512,1024]{1,0:T(8,128)(2,1)}, bf16[512,1024]{1,0:T(8,128)(2,1)}, u32[]{:S(2)}, u32[]{:S(2)}) collective-permute-start(bf16[512,1024]{1,0:T(8,128)(2,1)} %bitcast.8), channel_id=1, source_target_pairs={{8,0},{508,4},{16,8},{4,12},{24,16},{12,20},{32,24},{20,28},{40,32... | collective-permute-start | bytes 3145736 | tf_op jit(solution)/shard_map/ppermute | solution.py:320
  4.2 28.4 %collective-permute-start = (bf16[256,1024]{1,0:T(8,128)(2,1)}, bf16[256,1024]{1,0:T(8,128)(2,1)S(1)}, u32[]{:S(2)}, u32[]{:S(2)}) collective-permute-start(bf16[256,1024]{1,0:T(8,128)(2,1)} %bitcast.10), channel_id=1, source_target_pairs={{8,0},{508,4},{16,8},{4,12},{24,16},{12,20},{32,24},{20,28},{40,32... | collective-permute-start | bytes 1572872 | tf_op jit(solution)/shard_map/ppermute | solution.py:320
  7.4 1.2 %copy-start.2 = (bf16[1,512,1024]{2,1,0:T(8,128)(2,1)S(1)}, bf16[1,512,1024]{2,1,0:T(8,128)(2,1)}, u32[]{:S(2)}) copy-start(bf16[1,512,1024]{2,1,0:T(8,128)(2,1)} %param.4) | copy-start | bytes 3145732
  8.6 1.0 %copy-start.3 = (bf16[1,256,1024]{2,1,0:T(8,128)(2,1)S(1)}, bf16[1,256,1024]{2,1,0:T(8,128)(2,1)}, u32[]{:S(2)}) copy-start(bf16[1,256,1024]{2,1,0:T(8,128)(2,1)} %param.5) | copy-start | bytes 1572868
  11.7 34.9 %collective-permute-start.2 = (bf16[768,1024]{1,0:T(8,128)(2,1)S(1)}, bf16[768,1024]{1,0:T(8,128)(2,1)S(1)}, u32[]{:S(2)}, u32[]{:S(2)}) collective-permute-start(bf16[768,1024]{1,0:T(8,128)(2,1)S(1)} %get-tuple-element.13.own), channel_id=1, source_target_pairs={{4,0},{0,4},{12,8},{8,12},{20,16},{16,20},{28,24},{24,28},{36,32},... | collective-permute-start | bytes 4718600 | tf_op jit(solution)/shard_map/ppermute | solution.py:320
  25.0 29.7 %collective-permute-start.5 = (bf16[768,1024]{1,0:T(8,128)(2,1)S(1)}, bf16[768,1024]{1,0:T(8,128)(2,1)}, u32[]{:S(2)}, u32[]{:S(2)}) collective-permute-start(bf16[768,1024]{1,0:T(8,128)(2,1)S(1)} %get-tuple-element.13.own), channel_id=1, source_target_pairs={{504,0},{12,4},{0,8},{20,12},{8,16},{28,20},{16,24},{36,28},{24,32... | collective-permute-start | bytes 4718600 | tf_op jit(solution)/shard_map/ppermute | solution.py:320
  33.3 0.8 %copy-start = (bf16[256,1024]{1,0:T(8,128)(2,1)}, bf16[256,1024]{1,0:T(8,128)(2,1)S(1)}, u32[]{:S(2)}) copy-start(bf16[256,1024]{1,0:T(8,128)(2,1)S(1)} %amp.1.amp_2) | copy-start | bytes 1572868
  34.1 12.5 %collective-permute-start.4 = (bf16[512,1024]{1,0:T(8,128)(2,1)}, bf16[512,1024]{1,0:T(8,128)(2,1)}, u32[]{:S(2)}, u32[]{:S(2)}) collective-permute-start(bf16[512,1024]{1,0:T(8,128)(2,1)} %collective-permute-done.3.near), channel_id=1, source_target_pairs={{4,0},{0,4},{12,8},{8,12},{20,16},{16,20},{28,24},{24,28},{36,32},... | collective-permute-start | bytes 3145736 | tf_op jit(solution)/shard_map/ppermute | solution.py:320
  42.6 4.0 %collective-permute-start.1 = (bf16[256,1024]{1,0:T(8,128)(2,1)}, bf16[256,1024]{1,0:T(8,128)(2,1)S(1)}, u32[]{:S(2)}, u32[]{:S(2)}) collective-permute-start(bf16[256,1024]{1,0:T(8,128)(2,1)} %copy-done), channel_id=1, source_target_pairs={{4,0},{0,4},{12,8},{8,12},{20,16},{16,20},{28,24},{24,28},{36,32},... | collective-permute-start | bytes 1572872 | tf_op jit(solution)/shard_map/ppermute | solution.py:320
  44.7 10.1 %copy-start.1 = (bf16[256,1024]{1,0:T(8,128)(2,1)S(1)}, bf16[256,1024]{1,0:T(8,128)(2,1)}, u32[]{:S(2)}) copy-start(bf16[256,1024]{1,0:T(8,128)(2,1)} %copy-done) | copy-start | bytes 1572868
